TPU v7x, 32 devices: a whole 2x2x4 slice. The times are simulated.
32 devices in a mesh: batch: 8 (over z, x), heads: 4 (over y, core).
Axes of the slice: x: 2, y: 2, z: 4, core: 2. Of those that a mesh axis runs over, the one named last changes fastest.
Arguments:
- tokens: bfloat16 [16384, 768], P('batch'), may hold values from -6 to 6
- w_query: bfloat16 [768, 768], P(None, 'heads'), may hold values from -0.21875 to 0.21875
- w_key: bfloat16 [768, 768], P(None, 'heads'), may hold values from -0.21875 to 0.21875
- w_value: bfloat16 [768, 768], P(None, 'heads'), may hold values from -0.375 to 0.375
- w_output: bfloat16 [768, 768], P('heads'), may hold values from -0.375 to 0.375
- gain_attn: bfloat16 [768], replicated, may hold values from 0.099609375 to 1.8984375
- gain_inner: bfloat16 [768], P('heads'), may hold values from 0.099609375 to 1.8984375
- gain_ffn: bfloat16 [768], replicated, may hold values from 0.099609375 to 1.8984375
- w_expand: bfloat16 [3072, 768], P(('batch', 'heads')), may hold values from -0.375 to 0.375
- w_reduce: bfloat16 [3072, 768], P(('batch', 'heads')), may hold values from -0.1875 to 0.1875
- gain_hidden: bfloat16 [3072], P(('batch', 'heads')), may hold values from 0.099609375 to 1.8984375
- cotangent: bfloat16 [16384, 768], P(('batch', 'heads')), may hold values from -6 to 6
- seq_length: int32 [29], replicated, may hold values from 512 to 2048, as said below
- seq_group: int32 [29], replicated, may hold values from 0 to 7, as said below
Outputs:
- output: bfloat16 [16384, 768], P(('batch', 'heads'))
- grad_tokens: bfloat16 [16384, 768], P(('batch', 'heads'))
- grad_query: float32 [768, 768], P(None, 'heads')
- grad_key: float32 [768, 768], P(None, 'heads')
- grad_value: float32 [768, 768], P(None, 'heads')
- grad_output: float32 [768, 768], P('heads')
- grad_attn: float32 [768], replicated
- grad_inner: float32 [768], P('heads')
- grad_ffn: float32 [768], replicated
- grad_expand: float32 [3072, 768], P(('batch', 'heads'))
- grad_reduce: float32 [3072, 768], P(('batch', 'heads'))
- grad_hidden: float32 [3072], P(('batch', 'heads'))
Inputs may be any that keep to these rules, and one draw needn't show every extreme that they name: `seq_length`: each sequence has 512 or 2048 tokens; exactly 1 have 2048. `seq_group`: the sequences of each group have 2048 tokens together; 1 group hold one sequence of 2048 each.
All inputs are finite; a program needn't handle non-finite values.
Results may differ from a plain program's by a relative error of at most 0.018.
Values may be sent and summed in bfloat16 or wider, within the bound.
No kernel may reach another device: no remote copies, remote signals or barrier semaphores. Data moves between devices by JAX's collectives and lax.ppermute only.
A program may use at most 256 MiB of HBM per device.

v0:
```python
from functools import partial

import jax
import jax.numpy as jnp
from jax import lax
from jax.sharding import PartitionSpec as P

HD = 64
SHORT = 512


EPSILON = 1e-05
MASKED = -1e30
CONTRACT_ROWS = (((0,), (0,)), ((), ()))
CONTRACT_COLS = (((1,), (1,)), ((), ()))


def normalize(values):
    average = jnp.mean(values, axis=-1, keepdims=True)
    centred = values - average
    factor = lax.rsqrt(jnp.mean(centred * centred, axis=-1, keepdims=True) + EPSILON)
    return (centred * factor, factor)


def norm_back(grad_hat, normed, factor):
    return factor * (
        grad_hat
        - jnp.mean(grad_hat, axis=-1, keepdims=True)
        - normed * jnp.mean(grad_hat * normed, axis=-1, keepdims=True)
    )


def gelu_exact(values):
    return jax.nn.gelu(values, approximate=False)


def block_rows(values, index):
    return values[index * SHORT : (index + 1) * SHORT]


def visit(query_index, key_index, update, status, reaches):
    if key_index == query_index:
        return update(status)
    return lax.cond(reaches(query_index, key_index), update, lambda unchanged: unchanged, status)


def body(
    tokens,
    w_query,
    w_key,
    w_value,
    w_output,
    gain_attn,
    gain_inner,
    gain_ffn,
    w_expand,
    w_reduce,
    gain_hidden,
    cotangent,
    seq_length,
    seq_group,
):
    group_rows, model_width = tokens.shape
    local_width = w_query.shape[1]
    head_count = local_width // HD
    quarter = cotangent.shape[0]
    blocks = group_rows // SHORT
    score_scale = HD ** (-0.5)
    offset = lax.axis_index("heads") * quarter
    places = jnp.arange(group_rows, dtype=jnp.int32)
    mine_lengths = jnp.where(seq_group == lax.axis_index("batch"), seq_length, 0)
    finish = jnp.cumsum(mine_lengths)
    segment = jnp.sum((finish[None, :] <= places[:, None]).astype(jnp.int32), axis=1)

    def reaches(query_index, key_index):
        return segment[(key_index + 1) * SHORT - 1] >= segment[query_index * SHORT]

    source = tokens.astype(jnp.float32)
    pre_hat, pre_factor = normalize(source)
    attn_gain = gain_attn.astype(jnp.float32)
    pre_low = (pre_hat * attn_gain).astype(jnp.bfloat16)

    def project(weight):
        product = jnp.dot(pre_low, weight, preferred_element_type=jnp.float32)
        return product.astype(jnp.bfloat16).reshape(group_rows, head_count, HD)

    queries = project(w_query)
    key_low = project(w_key)
    value_low = project(w_value)

    def scores_of(query_index, key_index):
        raw_scores = (
            jnp.einsum(
                "qhd,khd->hqk",
                block_rows(queries, query_index),
                block_rows(key_low, key_index),
                preferred_element_type=jnp.float32,
            )
            * score_scale
        )
        same_segment = (
            block_rows(segment, query_index)[:, None] == block_rows(segment, key_index)[None, :]
        )
        earlier = block_rows(places, key_index)[None, :] <= block_rows(places, query_index)[:, None]
        return jnp.where((same_segment & earlier)[None], raw_scores, MASKED)

    def step_max(query_index, key_index, status):
        running, summed_exp = status
        scores = scores_of(query_index, key_index)
        newest = jnp.maximum(running, jnp.max(scores, axis=-1))
        summed_exp = summed_exp * jnp.exp(running - newest) + jnp.sum(
            jnp.exp(scores - newest[..., None]), axis=-1
        )
        return (newest, summed_exp)

    def step_out(query_index, key_index, logsum, status):
        weights_low = jnp.exp(scores_of(query_index, key_index) - logsum[..., None]).astype(
            jnp.bfloat16
        )
        return status + jnp.einsum(
            "hqk,khd->qhd",
            weights_low,
            block_rows(value_low, key_index),
            preferred_element_type=jnp.float32,
        )

    logsums = []
    out_blocks = []
    for query_index in range(blocks):
        visit_order = [query_index] + list(range(query_index))
        status = (
            jnp.full((head_count, SHORT), MASKED, jnp.float32),
            jnp.zeros((head_count, SHORT), jnp.float32),
        )
        for key_index in visit_order:
            status = visit(
                query_index, key_index, partial(step_max, query_index, key_index), status, reaches
            )
        logsum = status[0] + jnp.log(status[1])
        summed = jnp.zeros((SHORT, head_count, HD), jnp.float32)
        for key_index in visit_order:
            summed = visit(
                query_index,
                key_index,
                partial(step_out, query_index, key_index, logsum),
                summed,
                reaches,
            )
        logsums.append(logsum)
        out_blocks.append(summed)
    attended = jnp.concatenate(out_blocks, axis=0).reshape(group_rows, local_width)
    row_sum, row_square = lax.psum(
        (jnp.sum(attended, axis=1), jnp.sum(attended * attended, axis=1)), "heads"
    )
    average = row_sum[:, None] / model_width
    centred = attended - average
    spread = row_square[:, None] / model_width - average * average
    inner_factor = lax.rsqrt(spread + EPSILON)
    inner_hat = centred * inner_factor
    inner_gain = gain_inner.astype(jnp.float32)
    inner_low = (inner_hat * inner_gain).astype(jnp.bfloat16)
    branch = lax.psum_scatter(
        jnp.dot(inner_low, w_output, preferred_element_type=jnp.float32),
        "heads",
        scatter_dimension=0,
        tiled=True,
    )
    middle = lax.dynamic_slice_in_dim(source, offset, quarter, 0) + branch
    mid_hat, mid_factor = normalize(middle)
    mid_gain = gain_ffn.astype(jnp.float32)
    mid_low = (mid_hat * mid_gain).astype(jnp.bfloat16)
    upstream = cotangent.astype(jnp.float32)
    expand_all, reduce_all, hidden_gain = (
        lax.all_gather(w_expand, ("batch", "heads"), axis=0, tiled=True),
        lax.all_gather(w_reduce, ("batch", "heads"), axis=0, tiled=True),
        lax.all_gather(gain_hidden, ("batch", "heads"), axis=0, tiled=True),
    )
    hidden = lax.dot_general(mid_low, expand_all, CONTRACT_COLS, preferred_element_type=jnp.float32)
    activated, gelu_back = jax.vjp(gelu_exact, hidden)
    act_hat, act_factor = normalize(activated)
    hidden_gain32 = hidden_gain.astype(jnp.float32)
    post_low = (act_hat * hidden_gain32).astype(jnp.bfloat16)
    output = (middle + jnp.dot(post_low, reduce_all, preferred_element_type=jnp.float32)).astype(
        jnp.bfloat16
    )
    grad_reduce = lax.dot_general(
        post_low, cotangent, CONTRACT_ROWS, preferred_element_type=jnp.float32
    )
    grad_post = lax.dot_general(
        cotangent, reduce_all, CONTRACT_COLS, preferred_element_type=jnp.float32
    )
    grad_hidden_gain = jnp.sum(grad_post * act_hat, axis=0)
    grad_gelu = norm_back(grad_post * hidden_gain32, act_hat, act_factor)
    hidden_grad_low = gelu_back(grad_gelu)[0].astype(jnp.bfloat16)
    grad_expand = lax.dot_general(
        hidden_grad_low, mid_low, CONTRACT_ROWS, preferred_element_type=jnp.float32
    )
    mid_grad = jnp.dot(hidden_grad_low, expand_all, preferred_element_type=jnp.float32)
    expand_shard, reduce_shard, hidden_shard = (
        lax.psum_scatter(grad_expand, ("batch", "heads"), scatter_dimension=0, tiled=True),
        lax.psum_scatter(grad_reduce, ("batch", "heads"), scatter_dimension=0, tiled=True),
        lax.psum_scatter(grad_hidden_gain, ("batch", "heads"), scatter_dimension=0, tiled=True),
    )
    grad_ffn_part = jnp.sum(mid_grad * mid_hat, axis=0)
    middle_grad = upstream + norm_back(mid_grad * mid_gain, mid_hat, mid_factor)
    branch_grad = lax.all_gather(middle_grad.astype(jnp.bfloat16), "heads", axis=0, tiled=True)
    grad_w_output = lax.dot_general(
        inner_low, branch_grad, CONTRACT_ROWS, preferred_element_type=jnp.float32
    )
    inner_grad = lax.dot_general(
        branch_grad, w_output, CONTRACT_COLS, preferred_element_type=jnp.float32
    )
    grad_inner_part = jnp.sum(inner_grad * inner_hat, axis=0)
    scaled_grad = inner_grad * inner_gain
    grad_mean_sum, grad_cross_sum, grad_ffn_heads = lax.psum(
        (jnp.sum(scaled_grad, axis=1), jnp.sum(scaled_grad * inner_hat, axis=1), grad_ffn_part),
        "heads",
    )
    attended_grad = inner_factor * (
        scaled_grad
        - grad_mean_sum[:, None] / model_width
        - inner_hat * grad_cross_sum[:, None] / model_width
    )
    attended_grad_low = attended_grad.astype(jnp.bfloat16).reshape(group_rows, head_count, HD)

    def step_delta(query_index, key_index, logsum, status):
        weights_full = jnp.exp(scores_of(query_index, key_index) - logsum[..., None])
        weights_grad = jnp.einsum(
            "qhd,khd->hqk",
            block_rows(attended_grad_low, query_index),
            block_rows(value_low, key_index),
            preferred_element_type=jnp.float32,
        )
        return status + jnp.sum(weights_full * weights_grad, axis=-1)

    def step_grad(query_index, key_index, logsum, row_delta, status):
        query_acc, key_acc, value_acc = status
        weights_full = jnp.exp(scores_of(query_index, key_index) - logsum[..., None])
        grad_block = block_rows(attended_grad_low, query_index)
        weights_grad = jnp.einsum(
            "qhd,khd->hqk",
            grad_block,
            block_rows(value_low, key_index),
            preferred_element_type=jnp.float32,
        )
        score_grad = (weights_full * (weights_grad - row_delta[..., None])).astype(jnp.bfloat16)
        weights_low = weights_full.astype(jnp.bfloat16)
        query_acc = (
            query_acc
            + jnp.einsum(
                "hqk,khd->qhd",
                score_grad,
                block_rows(key_low, key_index),
                preferred_element_type=jnp.float32,
            )
            * score_scale
        )
        key_acc = (
            key_acc
            + jnp.einsum(
                "hqk,qhd->khd",
                score_grad,
                block_rows(queries, query_index),
                preferred_element_type=jnp.float32,
            )
            * score_scale
        )
        value_acc = value_acc + jnp.einsum(
            "hqk,qhd->khd", weights_low, grad_block, preferred_element_type=jnp.float32
        )
        return (query_acc, key_acc, value_acc)

    zero_block = jnp.zeros((SHORT, head_count, HD), jnp.float32)
    key_grads = [zero_block for unused_index in range(blocks)]
    value_grads = [zero_block for unused_index in range(blocks)]
    query_grads = []
    for query_index in range(blocks):
        visit_order = [query_index] + list(range(query_index))
        row_delta = jnp.zeros((head_count, SHORT), jnp.float32)
        for key_index in visit_order:
            row_delta = visit(
                query_index,
                key_index,
                partial(step_delta, query_index, key_index, logsums[query_index]),
                row_delta,
                reaches,
            )
        query_acc = zero_block
        for key_index in visit_order:
            query_acc, key_grads[key_index], value_grads[key_index] = visit(
                query_index,
                key_index,
                partial(step_grad, query_index, key_index, logsums[query_index], row_delta),
                (query_acc, key_grads[key_index], value_grads[key_index]),
                reaches,
            )
        query_grads.append(query_acc)

    def flat_low(parts):
        return jnp.concatenate(parts, axis=0).reshape(group_rows, local_width).astype(jnp.bfloat16)

    query_grad_low = flat_low(query_grads)
    key_grad_low = flat_low(key_grads)
    value_grad_low = flat_low(value_grads)
    grad_w_query = lax.dot_general(
        pre_low, query_grad_low, CONTRACT_ROWS, preferred_element_type=jnp.float32
    )
    grad_w_key = lax.dot_general(
        pre_low, key_grad_low, CONTRACT_ROWS, preferred_element_type=jnp.float32
    )
    grad_w_value = lax.dot_general(
        pre_low, value_grad_low, CONTRACT_ROWS, preferred_element_type=jnp.float32
    )
    pre_grad = lax.dot_general(
        query_grad_low, w_query, CONTRACT_COLS, preferred_element_type=jnp.float32
    )
    pre_grad = pre_grad + lax.dot_general(
        key_grad_low, w_key, CONTRACT_COLS, preferred_element_type=jnp.float32
    )
    pre_grad = pre_grad + lax.dot_general(
        value_grad_low, w_value, CONTRACT_COLS, preferred_element_type=jnp.float32
    )
    grad_attn_part = jnp.sum(pre_grad * pre_hat, axis=0)
    attn_tiled = jnp.broadcast_to(grad_attn_part[None, :], (lax.axis_size("heads"), model_width))
    input_part = norm_back(pre_grad * attn_gain, pre_hat, pre_factor)
    input_share, attn_heads = (
        lax.psum_scatter(
            input_part.astype(jnp.bfloat16), "heads", scatter_dimension=0, tiled=True
        ).astype(jnp.float32),
        lax.psum_scatter(
            attn_tiled.astype(jnp.bfloat16), "heads", scatter_dimension=0, tiled=True
        ).astype(jnp.float32),
    )
    grad_tokens = (middle_grad + input_share).astype(jnp.bfloat16)
    attn_totals = lax.psum(
        (
            grad_w_query,
            grad_w_key,
            grad_w_value,
            grad_w_output,
            grad_inner_part,
            attn_heads[0],
            grad_ffn_heads,
        ),
        "batch",
    )
    return (
        output,
        grad_tokens,
        attn_totals[0],
        attn_totals[1],
        attn_totals[2],
        attn_totals[3],
        attn_totals[5],
        attn_totals[4],
        attn_totals[6],
        expand_shard,
        reduce_shard,
        hidden_shard,
    )


def solution(mesh):
    return jax.shard_map(
        body,
        mesh=mesh,
        in_specs=(
            P("batch", None),
            P(None, "heads"),
            P(None, "heads"),
            P(None, "heads"),
            P("heads", None),
            P(),
            P("heads"),
            P(),
            P(("batch", "heads"), None),
            P(("batch", "heads"), None),
            P(("batch", "heads")),
            P(("batch", "heads"), None),
            P(),
            P(),
        ),
        out_specs=(
            P(("batch", "heads"), None),
            P(("batch", "heads"), None),
            P(None, "heads"),
            P(None, "heads"),
            P(None, "heads"),
            P("heads", None),
            P(),
            P("heads"),
            P(),
            P(("batch", "heads"), None),
            P(("batch", "heads"), None),
            P(("batch", "heads")),
        ),
        check_vma=False,
    )
```

profile of v0, /device:TPU:0, one launch (start us, length us, event | category | flops | bytes accessed | tf_op | source)
XLA Modules:
  0.0 830.5 jit_solution(9232196367520181172)
XLA Ops:
  33.6 3.7 convolution_bitcast_fusion.3
  41.7 3.6 convolution_bitcast_fusion.4
  52.5 3.7 convolution_bitcast_fusion.5
  61.8 13.2 %all-reduce.6 = (f32[2048]{0:T(1024)S(1)}, f32[2048]{0:T(1024)S(1)}) all-reduce(f32[2048]{0:T(1024)S(1)} %get-tuple-element.937, f32[2048]{0:T(1024)S(1)} %get-tuple-element.936), channel_id=1, replica_groups=mesh['batch'=8,'heads'=4] {'heads'}, use_global_device_ids=true, to_apply=%region_51.52 | all-reduce | flops 4096 | bytes 32768 | tf_op jit(solution)/shard_map/psum | solution.py:152
  77.8 3.8 fusion.287
  82.8 3.2 convert_element_type.216
  86.3 82.3 %all-reduce = bf16[3072]{0:T(1024)(128)(2,1)S(1)} all-reduce(bf16[3072]{0:T(1024)(128)(2,1)S(1)} %dynamic-update-slice), channel_id=1, replica_groups=mesh['batch'=8,'heads'=4] {'batch','heads'}, use_global_device_ids=true, to_apply=%add | all-reduce | flops 3072 | bytes 12288
  168.6 14.8 %reduce-scatter.5.cloned.1.call-done = f32[512,768]{1,0:T(8,128)} async-done(((f32[2048,768]{1,0:T(8,128)}), f32[512,768]{1,0:T(8,128)}) %reduce-scatter.5.cloned.1.call-update) | async-done | bytes 1572880 | tf_op jit(solution)/shard_map/reduce_scatter | solution.py:162
  185.9 30.7 %all-gather.4.cloned.1.call-done = bf16[3072,768]{1,0:T(8,128)(2,1)} async-done(((bf16[96,768]{1,0:T(8,128)(2,1)}), bf16[3072,768]{1,0:T(8,128)(2,1)}) %all-gather.4.cloned.1.call-update) | async-done | bytes 4718608 | tf_op jit(solution)/shard_map/all_gather | solution.py:174
  216.6 19.7 %fusion.301 = (f32[512]{0:T(512)S(1)}, f32[512,3072]{1,0:T(8,128)S(1)}, f32[512,3072]{1,0:T(8,128)}, f32[512,3072]{1,0:T(8,128)}) fusion(bf16[3072,768]{1,0:T(8,128)(2,1)} %all-gather.4.cloned.1.call-done, f32[512,768]{1,0:T(8,128)S(1)} %get-tuple-element.956, f32[768]{0:T(1024)S(1)} %convert_element_type.241, f32[512]{0:T(512)S(1)} %add_rsqrt_fusion.3, ...), kind=kOutput, calls=%fused_computation.453 | convolution fusion | flops 2519727616 | bytes 25175040 | tf_op jit(solution)/shard_map/dot_general | solution.py:178
  239.0 42.9 %all-gather.6.cloned.1.call-done = bf16[3072,768]{1,0:T(8,128)(2,1)} async-done(((bf16[96,768]{1,0:T(8,128)(2,1)}), bf16[3072,768]{1,0:T(8,128)(2,1)}) %all-gather.6.cloned.1.call-update) | async-done | bytes 4718608 | tf_op jit(solution)/shard_map/all_gather | solution.py:175
  281.9 7.6 multiply_reduce_fusion.6
  289.5 8.1 add_convert_fusion
  297.6 7.0 multiply_reduce_fusion.18
  306.7 26.9 %all-gather.8.cloned.1.call-done = bf16[2048,768]{1,0:T(8,128)(2,1)} async-done(((bf16[512,768]{1,0:T(8,128)(2,1)}), bf16[2048,768]{1,0:T(8,128)(2,1)}) %all-gather.8.cloned.1.call-update) | async-done | bytes 3145744 | tf_op jit(solution)/shard_map/all_gather | solution.py:206
  333.6 4.9 multiply_reduce_fusion.19
  338.5 11.8 %all-reduce.5 = (f32[2048]{0:T(1024)S(1)}, f32[2048]{0:T(1024)}, f32[768]{0:T(1024)}) all-reduce(f32[2048]{0:T(1024)S(1)} %get-tuple-element.933, f32[2048]{0:T(1024)S(1)} %get-tuple-element.935, f32[768]{0:T(1024)} %get-tuple-element.930), channel_id=1, replica_groups=mesh['batch'=8,'heads'=4] {'heads'}, use_global_device_ids=true, to_apply=%region_64.65 | all-reduce | flops 4864 | bytes 38912 | tf_op jit(solution)/shard_map/psum | solution.py:215
  366.3 3.8 multiply_convert_fusion.11
  377.3 3.9 multiply_convert_fusion.10
  389.5 2.9 multiply_convert_fusion.9
  398.3 7.4 conditional.47
  413.2 3.7 multiply_reduce_fusion.7
  416.9 3.4 multiply_convert_fusion.6
  430.2 8.3 %fusion.296 = f32[3072,768]{1,0:T(8,128)} fusion(bf16[512,3072]{1,0:T(8,128)(2,1)} %copy-done.55, f32[512,768]{1,0:T(8,128)S(1)} %copy-done.27, f32[768]{0:T(1024)S(1)} %convert_element_type.241, f32[512]{0:T(512)S(1)} %copy-done.112, f32[512]{0:T(512)S(1)} %broadcast_multiply_fusion.10), kind=kOutput, calls=%fused_computation.448 | convolution fusion | flops 2417491968 | bytes 14162944 | tf_op jit(solution)/shard_map/dot_general | solution.py:195
  439.7 9.3 %fusion.299 = f32[3072,768]{1,0:T(8,128)} fusion(bf16[512,768]{1,0:T(8,128)(2,1)S(1)} %copy-done.77, f32[512,3072]{1,0:T(8,128)} %copy-done.19, f32[3072]{0:T(1024)S(1)} %convert_element_type.243, f32[512]{0:T(512)S(1)} %add_rsqrt_fusion.2, f32[512]{0:T(512)S(1)} %broadcast_multiply_fusion.7), kind=kOutput, calls=%fused_computation.451 | convolution fusion | flops 2422210560 | bytes 16531456 | tf_op jit(solution)/shard_map/dot_general | solution.py:186
  450.3 94.1 %all-reduce.2 = f32[3072]{0:T(1024)S(1)} all-reduce(f32[3072]{0:T(1024)S(1)} %copy-done.110), channel_id=7, replica_groups=mesh['batch'=8,'heads'=4] {'batch','heads'}, use_global_device_ids=true, to_apply=%region_117.118.clone | all-reduce | flops 3072 | bytes 24576
  545.0 8.4 %add_convert_fusion.2 = bf16[512,768]{1,0:T(8,128)(2,1)} fusion(f32[512,768]{1,0:T(8,128)S(1)} %copy-done.27, bf16[3072,768]{1,0:T(8,128)(2,1)} %all-gather.6.cloned.1.call-done, f32[512,3072]{1,0:T(8,128)} %copy-done.19, f32[3072]{0:T(1024)S(1)} %convert_element_type.243, f32[512]{0:T(512)S(1)} %add_rsqrt_fusion.2, f32[512]{0:T(512)S(1)} %broadcast_multiply_fusion.7), kind=kOutput, calls=%fused_computation.367 | convolution fusion | flops 2422996992 | bytes 13385728 | tf_op jit(solution)/shard_map/dot_general | solution.py:183
  553.4 6.4 all-reduce.1
  560.5 22.4 %all-reduce.3 = (f32[768]{0:T(1024)}, f32[192]{0:T(256)}, f32[768]{0:T(1024)}) all-reduce(f32[768]{0:T(1024)S(1)} %fusion.284, f32[192]{0:T(256)S(1)} %copy-done.113, f32[768]{0:T(1024)S(1)} %copy-done.114), channel_id=1, replica_groups=mesh['batch'=8,'heads'=4] {'batch'}, use_global_device_ids=true, to_apply=%region_108.109 | all-reduce | flops 1728 | bytes 13824 | tf_op jit(solution)/shard_map/psum | solution.py:335
  585.1 26.5 %all-reduce.9.cloned.1.call-done = (f32[768,192]{0,1:T(8,128)}, f32[768,192]{0,1:T(8,128)}, f32[768,192]{0,1:T(8,128)}, f32[192,768]{1,0:T(8,128)}) async-done(((f32[768,192]{0,1:T(8,128)}, f32[768,192]{0,1:T(8,128)}, f32[768,192]{0,1:T(8,128)}, f32[192,768]{1,0:T(8,128)}), (f32[768,192]{0,1:T(8,128)}, f32[768,192]{0,1:T(8,128)}, f32[768,192]{0,1:T(8,128)}, ...) | async-done | bytes 2359312 | tf_op jit(solution)/shard_map/psum | solution.py:335
  611.7 63.7 %reduce-scatter.9.cloned.1.call-done = f32[96,768]{1,0:T(8,128)} async-done(((f32[3072,768]{1,0:T(8,128)}), f32[96,768]{1,0:T(8,128)}) %reduce-scatter.9.cloned.1.call-update) | async-done | bytes 294928 | tf_op jit(solution)/shard_map/reduce_scatter | solution.py:200
  675.3 140.8 %reduce-scatter.11.cloned.1.call-done = f32[96,768]{1,0:T(8,128)} async-done(((f32[3072,768]{1,0:T(8,128)}), f32[96,768]{1,0:T(8,128)}) %reduce-scatter.11.cloned.1.call-update) | async-done | bytes 294928 | tf_op jit(solution)/shard_map/reduce_scatter | solution.py:201
  (390 shorter events, 112.5 us)
Async XLA Ops:
  8.0 14.3 %copy-start = (bf16[768,192]{0,1:T(8,128)(2,1)S(1)}, bf16[768,192]{0,1:T(8,128)(2,1)}, u32[]{:S(2)}) copy-start(bf16[768,192]{0,1:T(8,128)(2,1)} %param.65) | copy-start | bytes 884740
  8.0 11.5 %copy-start.1 = (bf16[2048,768]{1,0:T(8,128)(2,1)S(1)}, bf16[2048,768]{1,0:T(8,128)(2,1)}, u32[]{:S(2)}) copy-start(bf16[2048,768]{1,0:T(8,128)(2,1)} %param.62) | copy-start | bytes 9437188
  8.0 175.4 %reduce-scatter.5.cloned.1.call-start = ((), (), s32[]{:S(2)}) async-start(), calls=%async_computation.4 | async-start | bytes 7864320 | tf_op jit(solution)/shard_map/reduce_scatter | solution.py:162
  22.3 4.5 copy-start.3
  25.9 7.4 copy-start.21
  28.0 5.3 copy-start.23
  48.1 4.3 copy-start.43
  81.6 135.0 %all-gather.4.cloned.1.call-start = ((), (), s32[]{:S(2)}) async-start(), calls=%async_computation.5 | async-start | bytes 4866048 | tf_op jit(solution)/shard_map/all_gather | solution.py:174
  82.2 199.7 %all-gather.6.cloned.1.call-start = ((), (), s32[]{:S(2)}) async-start(), calls=%async_computation.6 | async-start | bytes 4866048 | tf_op jit(solution)/shard_map/all_gather | solution.py:175
  82.8 250.8 %all-gather.8.cloned.1.call-start = ((), (), s32[]{:S(2)}) async-start(), calls=%async_computation.7 | async-start | bytes 3932160 | tf_op jit(solution)/shard_map/all_gather | solution.py:206
  185.5 119.0 %copy-start.26 = (f32[512,768]{1,0:T(8,128)}, f32[512,768]{1,0:T(8,128)S(1)}, u32[]{:S(2)}) copy-start(f32[512,768]{1,0:T(8,128)S(1)} %get-tuple-element.956) | copy-start | bytes 4718596
  185.9 118.7 %copy-start.111 = (f32[512]{0:T(512)}, f32[512]{0:T(512)S(1)}, u32[]{:S(2)}) copy-start(f32[512]{0:T(512)S(1)} %add_rsqrt_fusion.3) | copy-start | bytes 6148
  236.4 45.5 %copy-start.75 = (bf16[512,768]{1,0:T(8,128)(2,1)S(1)}, bf16[512,768]{1,0:T(8,128)(2,1)}, u32[]{:S(2)}) copy-start(bf16[512,768]{1,0:T(8,128)(2,1)} %param.73) | copy-start | bytes 2359300
  281.9 7.6 copy-start.20
  297.5 7.0 copy-start.55
  297.5 7.0 copy-start.76
  304.6 29.0 %copy-start.17 = (f32[2048,192]{0,1:T(8,128)S(1)}, f32[2048,192]{0,1:T(8,128)}, u32[]{:S(2)}) copy-start(f32[2048,192]{0,1:T(8,128)} %copy-done.16) | copy-start | bytes 4718596
  306.6 276.3 %reduce-scatter.7.cloned.1.call-start = ((), (), s32[]{:S(2)}) async-start(), calls=%async_computation.8 | async-start | bytes 3932160 | tf_op jit(solution)/shard_map/reduce_scatter | solution.py:327
  338.5 15.7 %copy-start.6 = (f32[3,512,512]{1,2,0:T(8,128)S(1)}, f32[3,512,512]{1,2,0:T(8,128)}, u32[]{:S(2)}) copy-start(f32[3,512,512]{1,2,0:T(8,128)} %copy-done.5) | copy-start | bytes 9437188
  353.4 12.7 %copy-start.56 = (bf16[2048,192]{0,1:T(8,128)(2,1)}, bf16[2048,192]{0,1:T(8,128)(2,1)S(1)}, u32[]{:S(2)}) copy-start(bf16[2048,192]{0,1:T(8,128)(2,1)S(1)} %multiply_convert_fusion.13) | copy-start | bytes 2359300
  354.1 8.8 %copy-start.87 = (bf16[512,192]{0,1:T(8,128)(2,1)}, bf16[512,192]{0,1:T(8,128)(2,1)S(1)}, u32[]{:S(2)}) copy-start(bf16[512,192]{0,1:T(8,128)(2,1)S(1)} %get-tuple-element.1117) | copy-start | bytes 589828
  366.3 5.0 copy-start.68
  377.3 5.1 copy-start.66
  377.3 8.3 copy-start.28
  412.4 4.5 copy-start.33
  420.4 191.3 %all-reduce.9.cloned.1.call-start = ((), (), s32[]{:S(2)}) async-start(), calls=%async_computation.11 | async-start | bytes 4718592 | tf_op jit(solution)/shard_map/psum | solution.py:335
  429.9 245.4 %reduce-scatter.9.cloned.1.call-start = ((), (), s32[]{:S(2)}) async-start(), calls=%async_computation.9 | async-start | bytes 9732096 | tf_op jit(solution)/shard_map/reduce_scatter | solution.py:200
  438.6 377.5 %reduce-scatter.11.cloned.1.call-start = ((), (), s32[]{:S(2)}) async-start(), calls=%async_computation.10 | async-start | bytes 9732096 | tf_op jit(solution)/shard_map/reduce_scatter | solution.py:201
  545.0 15.5 %copy-start.113 = (f32[192]{0:T(256)S(1)}, f32[192]{0:T(256)}, u32[]{:S(2)}) copy-start(f32[192]{0:T(256)} %get-tuple-element.932) | copy-start | bytes 2308
  545.0 15.5 %copy-start.114 = (f32[768]{0:T(1024)S(1)}, f32[768]{0:T(1024)}, u32[]{:S(2)}) copy-start(f32[768]{0:T(1024)} %get-tuple-element.947) | copy-start | bytes 9220
  545.0 37.9 %copy-start.48 = (f32[512,768]{1,0:T(8,128)S(1)}, f32[512,768]{1,0:T(8,128)}, u32[]{:S(2)}) copy-start(f32[512,768]{1,0:T(8,128)} %get-tuple-element.951) | copy-start | bytes 4718596
  611.7 210.2 %copy-start.89 = (f32[192,768]{1,0:T(8,128)S(1)}, f32[192,768]{1,0:T(8,128)}, u32[]{:S(2)}) copy-start(f32[192,768]{1,0:T(8,128)} %get-tuple-element.1232) | copy-start | bytes 1769476
  (82 other events, 183.4 us)
Sparse Core Ops, SparseCore 0:
  81.7 101.6 reduce-scatter.4
  306.8 26.7 all-gather.7
  420.5 91.8 reduce-scatter.6
  519.8 155.5 reduce-scatter.8
  681.7 134.4 reduce-scatter.10
Sparse Core Ops, SparseCore 1:
  85.4 131.2 all-gather.3
  219.8 62.0 all-gather.5
  430.0 181.6 all-reduce.8
where the time goes:
time: 840 us; the launch traced here: 830 us
  waiting for transfers between devices  348 us (41%)
  blocking collectives  230 us (27%)
  matrix products  131 us (16%)
  other arithmetic  55.6 us (7%)
  local copies, waits for them, and re-layouts  29.7 us (4%)
  between operations  25.2 us (3%)
  loops' own time  10.4 us (1%)
    unnamed x3, blocking collectives  183 us
    reduce_scatter x1, waiting for transfers between devices, body(): lax.psum_scatter(grad_reduce, ('batch', 'heads'), scatter_dimension=0, ti...  141 us
    reduce_scatter x1, waiting for transfers between devices, body(): lax.psum_scatter(grad_expand, ('batch', 'heads'), scatter_dimension=0, ti...  63.7 us
    all_gather x1, waiting for transfers between devices, body(): lax.all_gather(w_reduce, ('batch', 'heads'), axis=0, tiled=True)  42.9 us
    all_gather x1, waiting for transfers between devices, body(): lax.all_gather(w_expand, ('batch', 'heads'), axis=0, tiled=True)  30.7 us
    all_gather x1, waiting for transfers between devices, body(): lax.all_gather(middle_grad.astype(jnp.bfloat16), 'heads', axis=0, tiled=T...  26.9 us
    psum x1, waiting for transfers between devices, body(): lax.psum((grad_w_query, grad_w_key, grad_w_value, grad_w_output, grad_inn...  26.5 us
    unnamed x220, local copies, waits for them, and re-layouts  25.3 us
  transfers between devices with their start and end apart: 8, of which 7 were waited for; matrix products, arithmetic and copies ran while one was open for 8% of the time, Pallas kernels for 0%

commit v1 on v0

v1 whole, which is shorter than its diff:
```python
from functools import partial

import jax
import jax.numpy as jnp
from jax import lax
from jax.experimental import pallas as pl
from jax.experimental.pallas import tpu as pltpu
from jax.sharding import PartitionSpec as P

HD = 64
SHORT = 512
EPSILON = 1e-05
MASKED = -1e30
AXES = ("batch", "heads")
BF = jnp.bfloat16
F32 = jnp.float32
VMEM_LIMIT = 60 * 1024 * 1024


def dot(left, right, left_dim, right_dim):
    return lax.dot_general(
        left, right, (((left_dim,), (right_dim,)), ((), ())), preferred_element_type=F32
    )


def params(limit=VMEM_LIMIT):
    return pltpu.CompilerParams(vmem_limit_bytes=limit)


def vmem():
    return pl.BlockSpec(memory_space=pltpu.VMEM)


def smem():
    return pl.BlockSpec(memory_space=pltpu.SMEM)


def cost(flops, moved, special=0):
    return pl.CostEstimate(flops=flops, bytes_accessed=moved, transcendentals=special)


def attention_forward_kernel(
    flags, tokens, w_query, w_key, w_value, gain, pre, qkv, lse, *rest, n_own
):
    pieces, (w_t, s_buf, att_buf, acc) = rest[:n_own], rest[n_own:]
    rows, width = tokens.shape
    local = w_query.shape[1]
    heads = local // HD
    blocks = rows // SHORT
    tile = 64
    is_long, mine = flags[0], flags[1]
    gain_row = gain[...].astype(F32)

    for place, weight in enumerate((w_query, w_key, w_value)):
        w_t[place * local : (place + 1) * local, :] = weight[...].astype(F32).T.astype(BF)

    def norm_rows(step, unused):
        at = pl.ds(step * tile, tile)
        x = tokens[at, :].astype(F32)
        centred = x - jnp.mean(x, axis=1, keepdims=True)
        factor = lax.rsqrt(jnp.mean(centred * centred, axis=1, keepdims=True) + EPSILON)
        pre[at, :] = (centred * factor * gain_row).astype(BF)
        return unused

    lax.fori_loop(0, rows // tile, norm_rows, 0)

    for block in range(blocks):
        cols = slice(block * SHORT, (block + 1) * SHORT)
        product = dot(w_t[...], pre[cols, :], 1, 1)
        qkv[0:local, cols] = (product[0:local] * HD ** (-0.5)).astype(BF)
        qkv[local:, cols] = product[local:].astype(BF)

    def column_max(values):
        return jnp.max(values.reshape(values.shape[0] // 8, 8, SHORT), axis=0)

    def column_sum(values):
        return jnp.sum(values.reshape(values.shape[0] // 8, 8, SHORT), axis=0)

    key_place = lax.broadcasted_iota(jnp.int32, (SHORT, SHORT), 0)
    query_place = lax.broadcasted_iota(jnp.int32, (SHORT, SHORT), 1)

    def one_block(step, unused):
        head, block = step // blocks, step % blocks
        low = jnp.where(is_long > 0, 0, block)
        q_rows = pl.ds(pl.multiple_of(head * HD, HD), HD)
        k_rows = pl.ds(pl.multiple_of(local + head * HD, HD), HD)
        v_rows = pl.ds(pl.multiple_of(2 * local + head * HD, HD), HD)
        q_cols = pl.ds(pl.multiple_of(block * SHORT, SHORT), SHORT)
        q_t = qkv[q_rows, q_cols]

        def scores(index):
            cols = pl.ds(pl.multiple_of(index * SHORT, SHORT), SHORT)
            return dot(qkv[k_rows, cols], q_t, 0, 0)

        def visit(index, largest):
            s = scores(index)
            s_buf[pl.ds(pl.multiple_of(index * SHORT, SHORT), SHORT), :] = s
            return jnp.maximum(largest, column_max(s))

        largest = lax.fori_loop(low, block, visit, jnp.full((8, SHORT), MASKED, F32))
        s = jnp.where(key_place <= query_place, scores(block), MASKED)
        s_buf[pl.ds(pl.multiple_of(block * SHORT, SHORT), SHORT), :] = s
        largest = jnp.maximum(largest, column_max(s))
        top = jnp.max(largest, axis=0, keepdims=True)
        acc[...] = jnp.zeros_like(acc)

        def gather(index, total):
            cols = pl.ds(pl.multiple_of(index * SHORT, SHORT), SHORT)
            p = jnp.exp(s_buf[cols, :] - top)
            acc[...] += dot(qkv[v_rows, cols], p.astype(BF), 1, 0)
            return total + column_sum(p)

        total = lax.fori_loop(low, block + 1, gather, jnp.zeros((8, SHORT), F32))
        total = jnp.sum(total, axis=0, keepdims=True)
        att_buf[block, q_rows, :] = (acc[...] / total).astype(BF)
        lse[head, block] = jnp.broadcast_to(top + jnp.log(total), (8, SHORT))
        return unused

    lax.fori_loop(0, heads * blocks, one_block, 0)
    for place in range(n_own):
        pieces[place][...] = att_buf[mine ^ place]


def attention_forward(flags, tokens, w_query, w_key, w_value, gain, n_own):
    rows, width = tokens.shape
    local = w_query.shape[1]
    blocks = rows // SHORT
    heads = local // HD
    return pl.pallas_call(
        partial(attention_forward_kernel, n_own=n_own),
        out_shape=(
            jax.ShapeDtypeStruct((rows, width), BF),
            jax.ShapeDtypeStruct((3 * local, rows), BF),
            jax.ShapeDtypeStruct((heads, blocks, 8, SHORT), F32),
        )
        + (jax.ShapeDtypeStruct((local, SHORT), BF),) * n_own,
        in_specs=[smem()] + [vmem()] * 5,
        out_specs=[vmem()] * (3 + n_own),
        scratch_shapes=[
            pltpu.VMEM((3 * local, width), BF),
            pltpu.VMEM((rows, SHORT), F32),
            pltpu.VMEM((blocks, local, SHORT), BF),
            pltpu.VMEM((HD, SHORT), F32),
        ],
        compiler_params=params(),
        cost_estimate=cost(12_000_000_000, 10_000_000, 6_000_000),
        name="attention_forward",
    )(flags, tokens, w_query, w_key, w_value, gain)


def attention_backward_kernel(
    flags, qkv, lse, pre, w_query, w_key, w_value, *rest, n_own
):
    att, grads = rest[:n_own], rest[n_own : 2 * n_own]
    d_weight, attn_sum, sent, kept, ag, delta, d_qkv, dq, dk, dv = rest[2 * n_own :]
    rows, width = pre.shape
    local = w_query.shape[1]
    heads = local // HD
    blocks = rows // SHORT
    is_long, mine = flags[0], flags[1]

    for place in range(n_own):
        grad = grads[place][...]
        ag[mine ^ place] = grad
        product = grad.astype(F32) * att[place][...].astype(F32)
        for head in range(heads):
            summed = jnp.sum(product[head * HD : (head + 1) * HD], axis=0, keepdims=True)
            delta[head, mine ^ place] = jnp.broadcast_to(summed, (8, SHORT))

    key_place = lax.broadcasted_iota(jnp.int32, (SHORT, SHORT), 0)
    query_place = lax.broadcasted_iota(jnp.int32, (SHORT, SHORT), 1)

    def one_head(head, unused):
        q_rows = pl.ds(pl.multiple_of(head * HD, HD), HD)
        k_rows = pl.ds(pl.multiple_of(local + head * HD, HD), HD)
        v_rows = pl.ds(pl.multiple_of(2 * local + head * HD, HD), HD)
        dq[...] = jnp.zeros_like(dq)

        def one_key(block, unused):
            k_cols = pl.ds(pl.multiple_of(block * SHORT, SHORT), SHORT)
            k_t = qkv[k_rows, k_cols]
            v_t = qkv[v_rows, k_cols]

            def pair(index, masked):
                q_cols = pl.ds(pl.multiple_of(index * SHORT, SHORT), SHORT)
                q_t = qkv[q_rows, q_cols]
                grad = ag[index, q_rows, :]
                s = dot(k_t, q_t, 0, 0)
                p = jnp.exp(s - lse[head, index][0:1])
                if masked:
                    p = jnp.where(key_place <= query_place, p, 0.0)
                d_p = dot(v_t, grad, 0, 0)
                d_s = (p * (d_p - delta[head, index][0:1])).astype(BF)
                p = p.astype(BF)
                return (
                    dot(k_t, d_s, 1, 0),
                    dot(q_t, d_s, 1, 1),
                    dot(grad, p, 1, 1),
                )

            add_q, add_k, add_v = pair(block, True)
            dq[block] += add_q
            dk[...] = add_k
            dv[...] = add_v

            def visit(index, unused):
                add_q, add_k, add_v = pair(index, False)
                dq[index] += add_q
                dk[...] += add_k
                dv[...] += add_v
                return unused

            high = jnp.where(is_long > 0, blocks, block + 1)
            lax.fori_loop(block + 1, high, visit, 0)
            d_qkv[k_rows, k_cols] = dk[...].astype(BF)
            d_qkv[v_rows, k_cols] = dv[...].astype(BF)
            return unused

        lax.fori_loop(0, blocks, one_key, 0)
        for block in range(blocks):
            d_qkv[q_rows, block * SHORT : (block + 1) * SHORT] = (
                dq[block] * HD ** (-0.5)
            ).astype(BF)
        return unused

    lax.fori_loop(0, heads, one_head, 0)

    total = jnp.zeros((8, width), F32)
    for place, weight in enumerate((w_query, w_key, w_value)):
        at = slice(place * local, (place + 1) * local)
        product = dot(d_qkv[at, :], pre[...], 1, 0)
        d_weight[at, :] = product.astype(BF)
        cross = product * weight[...].astype(F32).T
        total = total + jnp.sum(cross.reshape(local // 8, 8, width), axis=0)
    attn_sum[...] = jnp.broadcast_to(jnp.sum(total, axis=0, keepdims=True), (8, width))

    half = n_own // 2
    for place in range(n_own):
        cols = pl.ds(pl.multiple_of((mine ^ place) * SHORT, SHORT), SHORT)
        grad = dot(w_query[...], d_qkv[0:local, cols], 1, 0)
        grad += dot(w_key[...], d_qkv[local : 2 * local, cols], 1, 0)
        grad += dot(w_value[...], d_qkv[2 * local :, cols], 1, 0)
        target = sent if place % 2 else kept
        target[place // 2] = grad.astype(BF)


def attention_backward(flags, qkv, lse, pre, w_query, w_key, w_value, att, grads):
    rows, width = pre.shape
    local = w_query.shape[1]
    blocks = rows // SHORT
    heads = local // HD
    n_own = len(att)
    half = max(n_own // 2, 1)
    return pl.pallas_call(
        partial(attention_backward_kernel, n_own=n_own),
        out_shape=(
            jax.ShapeDtypeStruct((3 * local, width), BF),
            jax.ShapeDtypeStruct((8, width), F32),
            jax.ShapeDtypeStruct((half, width, SHORT), BF),
            jax.ShapeDtypeStruct((half, width, SHORT), BF),
        ),
        in_specs=[smem()] + [vmem()] * (6 + 2 * n_own),
        out_specs=[vmem()] * 4,
        scratch_shapes=[
            pltpu.VMEM((blocks, local, SHORT), BF),
            pltpu.VMEM((heads, blocks, 8, SHORT), F32),
            pltpu.VMEM((3 * local, rows), BF),
            pltpu.VMEM((blocks, HD, SHORT), F32),
            pltpu.VMEM((HD, SHORT), F32),
            pltpu.VMEM((HD, SHORT), F32),
        ],
        compiler_params=params(),
        cost_estimate=cost(30_000_000_000, 16_000_000, 6_000_000),
        name="attention_backward",
    )(flags, qkv, lse, pre, w_query, w_key, w_value, *att, *grads)


def gelu_parts(h):
    phi = jnp.exp(h * h * (-0.5)) * 0.3989422804014327
    big = 0.5 * lax.erf(h * 0.7071067811865476) + 0.5
    return h * big, big + h * phi


def feed_forward_kernel(*refs, n_own):
    att, w_out, rest = refs[:n_own], refs[n_own : 2 * n_own], refs[2 * n_own :]
    (
        tokens,
        cotangent,
        gain_ffn,
        expand_a,
        expand_b,
        reduce_a,
        reduce_b,
        output,
        middle_grad,
        post,
        hidden_grad,
        mid_low,
        inner_t,
        branch_grad,
        ffn_sum,
    ) = rest[:15]
    grads = rest[15 : 15 + n_own]
    middle, act, slope, d_post, mid_acc = rest[15 + n_own :]
    rows, width = tokens.shape
    local = att[0].shape[0]
    chunk = SHORT
    tile = 16
    half = expand_a.shape[0]
    steps = half // chunk
    gain_row = gain_ffn[...].astype(F32)

    total = jnp.zeros((1, rows), F32)
    for piece in att:
        total = total + jnp.sum(piece[...].astype(F32), axis=0, keepdims=True)
    average = total / width
    square = jnp.zeros((1, rows), F32)
    for piece in att:
        centred = piece[...].astype(F32) - average
        square = square + jnp.sum(centred * centred, axis=0, keepdims=True)
    inner_factor = lax.rsqrt(square / width + EPSILON)
    for place, piece in enumerate(att):
        hat = (piece[...].astype(F32) - average) * inner_factor
        inner_t[place * local : (place + 1) * local, :] = hat.astype(BF)

    branch = dot(inner_t[0:local, :], w_out[0][...], 0, 0)
    for place in range(1, n_own):
        branch += dot(inner_t[place * local : (place + 1) * local, :], w_out[place][...], 0, 0)
    middle[...] = tokens[...].astype(F32) + branch

    def norm_tile(at):
        x = middle[at, :]
        centred = x - jnp.mean(x, axis=1, keepdims=True)
        factor = lax.rsqrt(jnp.mean(centred * centred, axis=1, keepdims=True) + EPSILON)
        return centred * factor, factor

    def norm_rows(step, unused):
        at = pl.ds(pl.multiple_of(step * tile, tile), tile)
        mid_low[at, :] = (norm_tile(at)[0] * gain_row).astype(BF)
        return unused

    lax.fori_loop(0, rows // tile, norm_rows, 0)

    for part, weight in enumerate((expand_a, expand_b)):
        def expand(step, unused, weight=weight, part=part):
            at = pl.ds(pl.multiple_of(step * chunk, chunk), chunk)
            to = pl.ds(pl.multiple_of(part * half + step * chunk, chunk), chunk)
            d_post[:, pl.ds(0, chunk)] = dot(mid_low[...], weight[at, :], 1, 1)

            def apply(row, unused):
                over = pl.ds(pl.multiple_of(row * tile, tile), tile)
                a, s = gelu_parts(d_post[over, pl.ds(0, chunk)])
                act[over, to] = a
                slope[over, to] = s.astype(BF)
                return unused

            lax.fori_loop(0, rows // tile, apply, 0)
            return unused

        lax.fori_loop(0, steps, expand, 0)

    hidden = 2 * half

    def act_tile(at):
        a = act[at, :]
        centred = a - jnp.sum(a, axis=1, keepdims=True) / hidden
        factor = lax.rsqrt(jnp.sum(centred * centred, axis=1, keepdims=True) / hidden + EPSILON)
        return centred * factor, factor

    def post_rows(step, unused):
        at = pl.ds(pl.multiple_of(step * tile, tile), tile)
        n, factor = act_tile(at)
        post[at, :] = n.astype(BF)
        mid_acc[at, 0:128] = jnp.broadcast_to(factor, (tile, 128))
        return unused

    lax.fori_loop(0, rows // tile, post_rows, 0)
    act_factor = mid_acc

    for part, weight in enumerate((reduce_a, reduce_b)):
        def up(step, unused, weight=weight, part=part):
            at = pl.ds(pl.multiple_of(step * chunk, chunk), chunk)
            to = pl.ds(pl.multiple_of(part * half + step * chunk, chunk), chunk)
            d_post[:, to] = dot(cotangent[...], weight[at, :], 1, 1)
            middle_out = dot(post[:, to], weight[at, :], 1, 0)
            act[:, 0:width] += middle_out
            return unused

        if part == 0:
            act[:, 0:width] = middle[...]
        lax.fori_loop(0, steps, up, 0)
    output[...] = act[:, 0:width].astype(BF)

    def back_rows(step, unused):
        at = pl.ds(pl.multiple_of(step * tile, tile), tile)
        e = d_post[at, :]
        n = post[at, :].astype(F32)
        mean_e = jnp.sum(e, axis=1, keepdims=True) / hidden
        mean_en = jnp.sum(e * n, axis=1, keepdims=True) / hidden
        factor = act_factor[at, 0:1]
        grad = factor * (e - mean_e - n * mean_en)
        hidden_grad[at, :] = (grad * slope[at, :].astype(F32)).astype(BF)
        return unused

    lax.fori_loop(0, rows // tile, back_rows, 0)

    mid_acc[...] = jnp.zeros_like(mid_acc)
    for part, weight in enumerate((expand_a, expand_b)):
        def down(step, unused, weight=weight, part=part):
            at = pl.ds(pl.multiple_of(step * chunk, chunk), chunk)
            to = pl.ds(pl.multiple_of(part * half + step * chunk, chunk), chunk)
            mid_acc[...] += dot(hidden_grad[:, to], weight[at, :], 1, 0)
            return unused

        lax.fori_loop(0, steps, down, 0)

    ffn_sum[...] = jnp.zeros_like(ffn_sum)

    def middle_rows(step, unused):
        at = pl.ds(pl.multiple_of(step * tile, tile), tile)
        n, factor = norm_tile(at)
        grad = mid_acc[at, :]
        cross = grad * n
        for part in range(tile // 8):
            ffn_sum[...] += cross[part * 8 : (part + 1) * 8]
        e = grad * gain_row
        back = factor * (
            e
            - jnp.mean(e, axis=1, keepdims=True)
            - n * jnp.mean(e * n, axis=1, keepdims=True)
        )
        full = cotangent[at, :].astype(F32) + back
        middle_grad[at, :] = full
        branch_grad[at, :] = full.astype(BF)
        return unused

    lax.fori_loop(0, rows // tile, middle_rows, 0)

    grad_sum = jnp.zeros((1, rows), F32)
    cross_sum = jnp.zeros((1, rows), F32)
    for place in range(n_own):
        e = dot(w_out[place][...], branch_grad[...], 1, 1)
        act[0:local, place * rows : (place + 1) * rows] = e
        grad_sum = grad_sum + jnp.sum(e, axis=0, keepdims=True)
        hat = (att[place][...].astype(F32) - average) * inner_factor
        cross_sum = cross_sum + jnp.sum(e * hat, axis=0, keepdims=True)
    for place in range(n_own):
        e = act[0:local, place * rows : (place + 1) * rows]
        hat = (att[place][...].astype(F32) - average) * inner_factor
        grad = inner_factor * (e - grad_sum / width - hat * (cross_sum / width))
        grads[place][...] = grad.astype(BF)


def feed_forward(att, w_out, tokens, cotangent, gain_ffn, expand, reduced):
    rows, width = tokens.shape
    hidden = 2 * expand[0].shape[0]
    n_own = len(att)
    local = att[0].shape[0]
    return pl.pallas_call(
        partial(feed_forward_kernel, n_own=n_own),
        out_shape=(
            jax.ShapeDtypeStruct((rows, width), BF),
            jax.ShapeDtypeStruct((rows, width), F32),
            jax.ShapeDtypeStruct((rows, hidden), BF),
            jax.ShapeDtypeStruct((rows, hidden), BF),
            jax.ShapeDtypeStruct((rows, width), BF),
            jax.ShapeDtypeStruct((n_own * local, rows), BF),
            jax.ShapeDtypeStruct((rows, width), BF),
            jax.ShapeDtypeStruct((8, width), F32),
        )
        + (jax.ShapeDtypeStruct((local, rows), BF),) * n_own,
        in_specs=[vmem()] * (2 * n_own + 7),
        out_specs=[vmem()] * (8 + n_own),
        scratch_shapes=[
            pltpu.VMEM((rows, width), F32),
            pltpu.VMEM((rows, hidden), F32),
            pltpu.VMEM((rows, hidden), BF),
            pltpu.VMEM((rows, hidden), F32),
            pltpu.VMEM((rows, width), F32),
        ],
        compiler_params=params(),
        cost_estimate=cost(20_000_000_000, 22_000_000, 4_000_000),
        name="feed_forward",
    )(*att, *w_out, tokens, cotangent, gain_ffn, *expand, *reduced)


def input_gradient_kernel(first, second, third, tokens, gain, middle_grad, out):
    width = first.shape[0]
    total = first[...].astype(F32) + second[...].astype(F32) + third[...].astype(F32)
    x = tokens[...].astype(F32)
    centred = x - jnp.mean(x, axis=1, keepdims=True)
    factor = lax.rsqrt(jnp.mean(centred * centred, axis=1, keepdims=True) + EPSILON)
    n = centred * factor
    e = total.T * gain[...].astype(F32)
    back = factor * (
        e - jnp.mean(e, axis=1, keepdims=True) - n * jnp.mean(e * n, axis=1, keepdims=True)
    )
    out[...] = (middle_grad[...] + back).astype(BF)


def input_gradient(terms, tokens, gain, middle_grad):
    return pl.pallas_call(
        input_gradient_kernel,
        out_shape=jax.ShapeDtypeStruct(tokens.shape, BF),
        in_specs=[vmem()] * 6,
        out_specs=vmem(),
        compiler_params=params(),
        cost_estimate=cost(10_000_000, 6_000_000),
        name="input_gradient",
    )(*terms, tokens, gain, middle_grad)


def body(
    tokens,
    w_query,
    w_key,
    w_value,
    w_output,
    gain_attn,
    gain_inner,
    gain_ffn,
    w_expand,
    w_reduce,
    gain_hidden,
    cotangent,
    seq_length,
    seq_group,
):
    n_batch, n_own = lax.axis_size("batch"), lax.axis_size("heads")
    n_all = n_batch * n_own
    mine = lax.axis_index("heads")
    quarter = cotangent.shape[0]
    width = tokens.shape[1]
    local = w_query.shape[1]

    def swap(value, bit):
        return lax.ppermute(value, AXES, [(i, i ^ bit) for i in range(n_all)])

    is_long = jnp.any((seq_group == lax.axis_index("batch")) & (seq_length > SHORT))
    flags = jnp.stack([is_long.astype(jnp.int32), mine.astype(jnp.int32)])

    def gathered(value, order):
        bits = [1 << b for b in range(n_all.bit_length() - 2, -1, -1)]
        value = value.reshape((1,) * (len(bits) - 1) + value.shape)
        for bit in order:
            value = jnp.concatenate([value, swap(value, bit)], axis=bits.index(bit))
        value = value.reshape(-1, value.shape[-1])
        return value, swap(value, 1)

    def scattered(kept, sent, order):
        bits = [1 << b for b in range(n_all.bit_length() - 2, -1, -1)]
        value = kept.astype(F32) + swap(sent, 1).astype(F32)
        value = value.reshape((2,) * (len(bits) - 1) + (-1, value.shape[-1]))
        for bit in reversed(order):
            axis = bits.index(bit)
            keep, send = (lax.slice_in_dim(value, i, i + 1, axis=axis) for i in (0, 1))
            value = keep + swap(send.astype(BF), bit).astype(F32)
        return value.reshape(-1, value.shape[-1])

    down = [1 << b for b in range(n_all.bit_length() - 2, 0, -1)]
    order_expand = down
    order_reduce = [2] + [b for b in down if b > 4] + [4]
    w_reduce_scaled = (w_reduce.astype(F32) * gain_hidden.astype(F32)[:, None]).astype(BF)
    w_output_scaled = (w_output.astype(F32) * gain_inner.astype(F32)[:, None]).astype(BF)
    expand = gathered(w_expand, order_expand)
    reduced = gathered(w_reduce_scaled, order_reduce)
    w_out = [w_output_scaled] + [swap(w_output_scaled, k) for k in range(1, n_own)]
    gain_attn_row = gain_attn[None, :]
    pre, qkv, lse, *pieces = attention_forward(
        flags, tokens, w_query, w_key, w_value, gain_attn_row, n_own
    )
    att = [pieces[0]] + [swap(pieces[k], k) for k in range(1, n_own)]
    own_tokens = lax.dynamic_slice_in_dim(tokens, mine * quarter, quarter, 0)
    (
        output,
        middle_grad,
        post,
        hidden_grad,
        mid_low,
        inner_t,
        branch_grad,
        ffn_sum,
        *att_grads,
    ) = feed_forward(att, w_out, own_tokens, cotangent, gain_ffn[None, :], expand, reduced)
    grads = [att_grads[0]] + [swap(att_grads[k], k) for k in range(1, n_own)]

    half = post.shape[1] // 2

    def outer(left, right):
        return dot(left, right, 0, 0).astype(BF)

    d_reduce = scattered(
        outer(post[:, :half], cotangent), outer(post[:, half:], cotangent), order_reduce
    )
    d_expand = scattered(
        outer(hidden_grad[:, :half], mid_low), outer(hidden_grad[:, half:], mid_low), order_expand
    )
    d_out = [
        dot(inner_t[k * local : (k + 1) * local], branch_grad, 1, 0) for k in range(n_own)
    ]
    d_own = d_out[0]
    for k in range(1, n_own):
        d_own = d_own + swap(d_out[k].astype(BF), k).astype(F32)

    d_qkv, attn_sum, sent, kept = attention_backward(
        flags, qkv, lse, pre, w_query, w_key, w_value, pieces, grads
    )
    came = swap(sent, 1)
    second = swap((kept[1].astype(F32) + came[1].astype(F32)).astype(BF), 2)
    grad_tokens = input_gradient(
        (kept[0], came[0], second), own_tokens, gain_attn_row, middle_grad
    )

    weights = jnp.concatenate([d_qkv, d_own.astype(BF)], axis=0)
    batch_bits = [b for b in (1 << i for i in range(n_all.bit_length() - 1)) if b >= n_own]
    share = weights.reshape((2,) * len(batch_bits) + (-1, width)).astype(F32)
    for axis, bit in enumerate(batch_bits):
        keep, send = (lax.slice_in_dim(share, i, i + 1, axis=axis) for i in (0, 1))
        index = (lax.axis_index("batch") >> axis) & 1
        keep, send = jnp.where(index == 0, keep, send), jnp.where(index == 0, send, keep)
        share = keep + swap(send.astype(BF), bit).astype(F32)
    share = share.astype(BF)
    for axis, bit in reversed(list(enumerate(batch_bits))):
        other = swap(share, bit)
        index = (lax.axis_index("batch") >> axis) & 1
        share = jnp.where(
            index == 0,
            jnp.concatenate([share, other], axis=axis),
            jnp.concatenate([other, share], axis=axis),
        )
    total = share.reshape(-1, width).astype(F32)
    small = jnp.stack([attn_sum[0], jnp.sum(ffn_sum, axis=0)])
    for bit in [1 << i for i in range(n_all.bit_length() - 1)]:
        small = small + swap(small, bit)
    g_out = total[3 * local :]
    return (
        output,
        grad_tokens,
        total[:local].T,
        total[local : 2 * local].T,
        total[2 * local : 3 * local].T,
        g_out * gain_inner.astype(F32)[:, None],
        small[0] / gain_attn.astype(F32),
        jnp.sum(g_out * w_output.astype(F32), axis=1),
        small[1],
        d_expand,
        d_reduce * gain_hidden.astype(F32)[:, None],
        jnp.sum(d_reduce * w_reduce.astype(F32), axis=1),
    )


def solution(mesh):
    both = P(AXES, None)
    return jax.shard_map(
        body,
        mesh=mesh,
        in_specs=(
            P("batch", None),
            P(None, "heads"),
            P(None, "heads"),
            P(None, "heads"),
            P("heads", None),
            P(),
            P("heads"),
            P(),
            both,
            both,
            P(AXES),
            both,
            P(),
            P(),
        ),
        out_specs=(
            both,
            both,
            P(None, "heads"),
            P(None, "heads"),
            P(None, "heads"),
            P("heads", None),
            P(),
            P("heads"),
            P(),
            both,
            both,
            P(AXES),
        ),
        check_vma=False,
    )
```

time: 840 us -> 385 us (0.46); the launches traced: 830 us -> 385 us
  blocking collectives: 230 us -> 0 us
  waiting for transfers between devices: 348 us -> 168 us
  matrix products: 131 us -> 10.9 us
  Pallas kernels: 0 us -> 102 us
  starting transfers between devices: 0.58 us -> 72.6 us
  other arithmetic: 55.6 us -> 16.6 us
  between operations: 25.2 us -> 2.05 us
  local copies, waits for them, and re-layouts: 29.7 us -> 12.9 us
  loops' own time: 10.4 us -> 0 us
    reduce_scatter x4 -> x0, waiting for transfers between devices: 219 us -> none  [the longest x1 141 us: body(): lax.psum_scatter(grad_reduce, ('batch', 'heads'), scatter_dimension=0, ti...]
    unnamed x3 -> x0, blocking collectives: 183 us -> none
    ppermute x0 -> x45, waiting for transfers between devices: none -> 168 us  [swap(): return lax.ppermute(value, AXES, [(i, i ^ bit) for i in range(n_all)])]
    dot_general x42 -> x8, matrix products: 131 us -> 10.9 us  [dot(): lax.dot_general(left, right, (((left_dim,), (right_dim,)), ((), ())), pre...]
    pallas_call x0 -> x4, Pallas kernels: none -> 102 us  [the longest x1 55.6 us: feed_forward(): pl.pallas_call(partial(feed_forward_kernel, n_own=n_own), out_shape=(jax....]
    all_gather x3 -> x0, waiting for transfers between devices: 101 us -> none  [the longest x1 42.9 us: body(): lax.all_gather(w_reduce, ('batch', 'heads'), axis=0, tiled=True)]
    ppermute x0 -> x45, starting transfers between devices: none -> 72.6 us  [swap(): return lax.ppermute(value, AXES, [(i, i ^ bit) for i in range(n_all)])]
    psum x3 -> x0, blocking collectives: 47.5 us -> none  [the longest x1 22.4 us: body(): lax.psum((grad_w_query, grad_w_key, grad_w_value, grad_w_output, grad_inn...]
  transfers between devices with their start and end apart: 8 -> 45, of which waited for: 7 -> 23; matrix products, arithmetic and copies ran while one was open for 8% -> 8% of each run, Pallas kernels for 0% -> 12%
where the time goes in v1:
time: 385 us
  waiting for transfers between devices  168 us (44%)
  Pallas kernels  102 us (26%)
  starting transfers between devices  72.6 us (19%)
  other arithmetic  16.6 us (4%)
  local copies, waits for them, and re-layouts  12.9 us (3%)
  matrix products  10.9 us (3%)
    ppermute x45, waiting for transfers between devices, swap(): return lax.ppermute(value, AXES, [(i, i ^ bit) for i in range(n_all)])  168 us
    ppermute x45, starting transfers between devices, swap(): return lax.ppermute(value, AXES, [(i, i ^ bit) for i in range(n_all)])  72.6 us
    pallas_call x1, Pallas kernels, feed_forward(): pl.pallas_call(partial(feed_forward_kernel, n_own=n_own), out_shape=(jax....  55.6 us
    pallas_call x1, Pallas kernels, attention_forward(): pl.pallas_call(partial(attention_forward_kernel, n_own=n_own), out_shape=...  21.6 us
    pallas_call x1, Pallas kernels, attention_backward(): pl.pallas_call(partial(attention_backward_kernel, n_own=n_own), out_shape...  20.5 us
    dot_general x8, matrix products, dot(): lax.dot_general(left, right, (((left_dim,), (right_dim,)), ((), ())), pre...  10.9 us
  transfers between devices with their start and end apart: 45, of which 23 were waited for; matrix products, arithmetic and copies ran while one was open for 8% of the time, Pallas kernels for 12%

profile of v1, /device:TPU:0, one launch (start us, length us, event | category | flops | bytes accessed | tf_op | source)
XLA Modules:
  0.0 385.0 jit_solution(10656907205354257872)
XLA Ops:
  2.4 3.0 collective-permute-start.11
  5.4 3.8 collective-permute-done.11
  9.3 2.9 collective-permute-start.12
  12.3 18.8 %collective-permute-done.6 = bf16[1,1,1,1,96,768]{5,4,3,2,1,0:T(8,128)(2,1)S(1)} collective-permute-done((bf16[1,1,1,1,96,768]{5,4,3,2,1,0:T(8,128)(2,1)}, bf16[1,1,1,1,96,768]{5,4,3,2,1,0:T(8,128)(2,1)S(1)}, u32[]{:S(2)}, u32[]{:S(2)}) %collective-permute-start.6) | collective-permute-done | bytes 147488 | tf_op jit(solution)/shard_map/ppermute | solution.py:537
  34.2 7.8 %collective-permute-done.7 = bf16[2,1,1,1,96,768]{5,4,3,2,1,0:T(8,128)(2,1)S(1)} collective-permute-done((bf16[2,1,1,1,96,768]{5,4,3,2,1,0:T(8,128)(2,1)S(1)}, bf16[2,1,1,1,96,768]{5,4,3,2,1,0:T(8,128)(2,1)S(1)}, u32[]{:S(2)}, u32[]{:S(2)}) %collective-permute-start.7) | collective-permute-done | bytes 294944 | tf_op jit(solution)/shard_map/ppermute | solution.py:537
  43.5 9.1 %collective-permute-done.13 = bf16[2,1,1,2,96,768]{5,4,3,2,1,0:T(8,128)(2,1)S(1)} collective-permute-done((bf16[2,1,1,2,96,768]{5,4,3,2,1,0:T(8,128)(2,1)S(1)}, bf16[2,1,1,2,96,768]{5,4,3,2,1,0:T(8,128)(2,1)S(1)}, u32[]{:S(2)}, u32[]{:S(2)}) %collective-permute-start.13) | collective-permute-done | bytes 589856 | tf_op jit(solution)/shard_map/ppermute | solution.py:537
  56.0 23.1 %collective-permute-done.14 = bf16[2,2,1,2,96,768]{5,4,3,2,1,0:T(8,128)(2,1)S(1)} collective-permute-done((bf16[2,2,1,2,96,768]{5,4,3,2,1,0:T(8,128)(2,1)S(1)}, bf16[2,2,1,2,96,768]{5,4,3,2,1,0:T(8,128)(2,1)S(1)}, u32[]{:S(2)}, u32[]{:S(2)}) %collective-permute-start.14) | collective-permute-done | bytes 1179680 | tf_op jit(solution)/shard_map/ppermute | solution.py:537
  87.3 21.6 %attention_forward.1 = (bf16[2048,768]{1,0:T(8,128)(2,1)}, bf16[576,2048]{1,0:T(8,128)(2,1)}, f32[3,4,8,512]{3,2,1,0:T(8,128)}, bf16[192,512]{1,0:T(8,128)(2,1)}...) custom-call(s32[2]{0:T(128)} %pad_add_fusion.flags, bf16[2048,768]{1,0:T(8,128)(2,1)} %tokens.1, ...), custom_call_target="tpu_custom_call" | custom-call | flops 12000000000 | bytes 10000000 | tf_op jit(solution)/shard_map/attention_forward/pallas_call | solution.py:129
  111.7 5.6 %collective-permute-done.1.refs_2_ = bf16[192,512]{1,0:T(8,128)(2,1)S(1)} collective-permute-done((bf16[192,512]{1,0:T(8,128)(2,1)}, bf16[192,512]{1,0:T(8,128)(2,1)S(1)}, u32[]{:S(2)}, u32[]{:S(2)}) %collective-permute-start.1) | collective-permute-done | bytes 196640 | tf_op jit(solution)/shard_map/ppermute | solution.py:537
  123.7 2.1 constant_dynamic-slice_fusion.refs_8_.tokens
  125.8 2.2 collective-permute-done.4.refs_6_
  128.0 4.5 %collective-permute-done.5.refs_7_ = bf16[192,768]{1,0:T(8,128)(2,1)} collective-permute-done((bf16[192,768]{1,0:T(8,128)(2,1)S(1)}, bf16[192,768]{1,0:T(8,128)(2,1)}, u32[]{:S(2)}, u32[]{:S(2)}) %collective-permute-start.5) | collective-permute-done | bytes 294944 | tf_op jit(solution)/shard_map/ppermute | solution.py:537
  132.4 55.6 %feed_forward.1 = (bf16[512,768]{1,0:T(8,128)(2,1)}, f32[512,768]{1,0:T(8,128)}, bf16[512,3072]{1,0:T(8,128)(2,1)}, bf16[512,3072]{1,0:T(8,128)(2,1)}, bf16[512,...) custom-call(bf16[192,512]{1,0:T(8,128)(2,1)} %get-tuple-element.35.r, ...), custom_call_target="tpu_custom_call" | custom-call | flops 20000000000 | bytes 22000000 | tf_op jit(solution)/shard_map/feed_forward/pallas_call | solution.py:459
  196.4 3.7 collective-permute-done.17.rest_6_
  200.1 3.1 collective-permute-done.18.rest_7_
  203.2 20.5 %attention_backward.1 = (bf16[576,768]{1,0:T(8,128)(2,1)}, f32[8,768]{1,0:T(8,128)}, bf16[2,768,512]{2,1,0:T(8,128)(2,1)}, bf16[2,768,512]{2,1,0:T(8,128)(2,1)}) custom-call(s32[2]{0:T(128)} %pad_add_fusion.flags, bf16[576,2048]{1,0:T(8,128)(2,1)} %get-tuple-element.40.qkv, f32[3,4,8,512]{3,2,1,0:T(8,128)} %get-tuple-element.41.lse, ...), custom_call_target="tpu_custom_call" | custom-call | flops 30000001024 | bytes 16000000 | tf_op jit(solution)/shard_map/attention_backward/pallas_call | solution.py:254
  232.5 10.2 %collective-permute-done.24 = bf16[1,2,2,96,768]{4,3,2,1,0:T(8,128)(2,1)S(1)} collective-permute-done((bf16[1,2,2,96,768]{4,3,2,1,0:T(8,128)(2,1)S(1)}, bf16[1,2,2,96,768]{4,3,2,1,0:T(8,128)(2,1)S(1)}, u32[]{:S(2)}, u32[]{:S(2)}) %collective-permute-start.24) | collective-permute-done | bytes 589856 | tf_op jit(solution)/shard_map/ppermute | solution.py:537
  242.8 29.0 %collective-permute-start.25 = (bf16[1,1,2,96,768]{4,3,2,1,0:T(8,128)(2,1)S(1)}, bf16[1,1,2,96,768]{4,3,2,1,0:T(8,128)(2,1)S(1)}, u32[]{:S(2)}, u32[]{:S(2)}) collective-permute-start(bf16[1,1,2,96,768]{4,3,2,1,0:T(8,128)(2,1)S(1)} %select_convert_fusion.1), channel_id=1, source_target_pairs={{0,8},{1,9},{2,10},{3,11},{4,12},{5,13},{6,14},{7,15},{8,0},{9,1},... | collective-permute-start | bytes 884744 | tf_op jit(solution)/shard_map/ppermute | solution.py:537
  275.3 3.3 collective-permute-done.25
  282.1 5.4 %collective-permute-done.26 = bf16[1,1,1,96,768]{4,3,2,1,0:T(8,128)(2,1)S(1)} collective-permute-done((bf16[1,1,1,96,768]{4,3,2,1,0:T(8,128)(2,1)S(1)}, bf16[1,1,1,96,768]{4,3,2,1,0:T(8,128)(2,1)S(1)}, u32[]{:S(2)}, u32[]{:S(2)}) %collective-permute-start.26) | collective-permute-done | bytes 147488 | tf_op jit(solution)/shard_map/ppermute | solution.py:537
  289.2 3.0 collective-permute-start.34
  292.2 3.8 collective-permute-done.27
  297.7 7.2 %collective-permute-done.28 = bf16[1,1,2,96,768]{4,3,2,1,0:T(8,128)(2,1)S(1)} collective-permute-done((bf16[1,1,2,96,768]{4,3,2,1,0:T(8,128)(2,1)S(1)}, bf16[1,1,2,96,768]{4,3,2,1,0:T(8,128)(2,1)S(1)}, u32[]{:S(2)}, u32[]{:S(2)}) %collective-permute-start.28) | collective-permute-done | bytes 294944 | tf_op jit(solution)/shard_map/ppermute | solution.py:537
  306.0 2.1 collective-permute-start.41
  312.6 9.0 %collective-permute-done.29 = bf16[1,2,2,96,768]{4,3,2,1,0:T(8,128)(2,1)S(1)} collective-permute-done((bf16[1,2,2,96,768]{4,3,2,1,0:T(8,128)(2,1)S(1)}, bf16[1,2,2,96,768]{4,3,2,1,0:T(8,128)(2,1)S(1)}, u32[]{:S(2)}, u32[]{:S(2)}) %collective-permute-start.29) | collective-permute-done | bytes 589856 | tf_op jit(solution)/shard_map/ppermute | solution.py:537
  321.8 23.1 %collective-permute-done.41 = bf16[2,2,1,2,96,768]{5,4,3,2,1,0:T(8,128)(2,1)S(1)} collective-permute-done((bf16[2,2,1,2,96,768]{5,4,3,2,1,0:T(8,128)(2,1)S(1)}, bf16[2,2,1,2,96,768]{5,4,3,2,1,0:T(8,128)(2,1)S(1)}, u32[]{:S(2)}, u32[]{:S(2)}) %collective-permute-start.41) | collective-permute-done | bytes 1179680 | tf_op jit(solution)/shard_map/ppermute | solution.py:537
  346.9 11.8 %collective-permute-done.42 = bf16[2,1,1,2,96,768]{5,4,3,2,1,0:T(8,128)(2,1)S(1)} collective-permute-done((bf16[2,1,1,2,96,768]{5,4,3,2,1,0:T(8,128)(2,1)S(1)}, bf16[2,1,1,2,96,768]{5,4,3,2,1,0:T(8,128)(2,1)S(1)}, u32[]{:S(2)}, u32[]{:S(2)}) %collective-permute-start.42) | collective-permute-done | bytes 589856 | tf_op jit(solution)/shard_map/ppermute | solution.py:537
  362.3 2.1 fusion.9
  365.3 4.6 %input_gradient.1 = bf16[512,768]{1,0:T(8,128)(2,1)} custom-call(bf16[768,512]{1,0:T(8,128)(2,1)} %slice_bitcast_fusion.1.first, bf16[768,512]{1,0:T(8,128)(2,1)} %slice_bitcast_fusion.second, bf16[768,512]{1,0:T(8,128)(2,1)} %copy-done.7, bf16[512,768]{1,0:T(8,128)(2,1)} %constant_dynamic-slice_fusion.refs_8_.tokens, bf16[1,768]{1,0:T(2,128)(2,1)} %broadcast_in_dim.4.gain, ...), custom_call_target="tpu_custom_call" | custom-call | flops 10000000 | bytes 6000000 | tf_op jit(solution)/shard_map/input_gradient/pallas_call | solution.py:502
  369.9 2.7 collective-permute-done.43
  376.3 2.5 collective-permute-done.44
  380.2 4.1 %collective-permute-done.39 = bf16[1,1,1,1,96,768]{5,4,3,2,1,0:T(8,128)(2,1)S(1)} collective-permute-done((bf16[1,1,1,1,96,768]{5,4,3,2,1,0:T(8,128)(2,1)S(1)}, bf16[1,1,1,1,96,768]{5,4,3,2,1,0:T(8,128)(2,1)S(1)}, u32[]{:S(2)}, u32[]{:S(2)}) %collective-permute-start.39) | collective-permute-done | bytes 147488 | tf_op jit(solution)/shard_map/ppermute | solution.py:537
  (196 shorter events, 71.7 us)
Async XLA Ops:
  9.3 23.5 %collective-permute-start.12 = (bf16[1,1,1,2,96,768]{5,4,3,2,1,0:T(8,128)(2,1)S(1)}, bf16[1,1,1,2,96,768]{5,4,3,2,1,0:T(8,128)(2,1)S(1)}, u32[]{:S(2)}, u32[]{:S(2)}) collective-permute-start(bf16[1,1,1,2,96,768]{5,4,3,2,1,0:T(8,128)(2,1)S(1)} %pad_maximum_fusion.7), channel_id=1, source_target_pairs={{0,16},{1,17},{2,18},{3,19},{4,20},{5,21},{6,22},{7,23},{8,24},{9,... | collective-permute-start | bytes 884744 | tf_op jit(solution)/shard_map/ppermute | solution.py:537
  12.1 18.9 %collective-permute-start.6 = (bf16[1,1,1,1,96,768]{5,4,3,2,1,0:T(8,128)(2,1)}, bf16[1,1,1,1,96,768]{5,4,3,2,1,0:T(8,128)(2,1)S(1)}, u32[]{:S(2)}, u32[]{:S(2)}) collective-permute-start(bf16[1,1,1,1,96,768]{5,4,3,2,1,0:T(8,128)(2,1)} %bitcast.51), channel_id=1, source_target_pairs={{0,16},{1,17},{2,18},{3,19},{4,20},{5,21},{6,22},{7,23},{8,24},{9,... | collective-permute-start | bytes 442376 | tf_op jit(solution)/shard_map/ppermute | solution.py:537
  32.0 10.0 %collective-permute-start.7 = (bf16[2,1,1,1,96,768]{5,4,3,2,1,0:T(8,128)(2,1)S(1)}, bf16[2,1,1,1,96,768]{5,4,3,2,1,0:T(8,128)(2,1)S(1)}, u32[]{:S(2)}, u32[]{:S(2)}) collective-permute-start(bf16[2,1,1,1,96,768]{5,4,3,2,1,0:T(8,128)(2,1)S(1)} %pad_maximum_fusion.6), channel_id=1, source_target_pairs={{0,8},{1,9},{2,10},{3,11},{4,12},{5,13},{6,14},{7,15},{8,0},{9,1},... | collective-permute-start | bytes 884744 | tf_op jit(solution)/shard_map/ppermute | solution.py:537
  32.8 19.8 %collective-permute-start.13 = (bf16[2,1,1,2,96,768]{5,4,3,2,1,0:T(8,128)(2,1)S(1)}, bf16[2,1,1,2,96,768]{5,4,3,2,1,0:T(8,128)(2,1)S(1)}, u32[]{:S(2)}, u32[]{:S(2)}) collective-permute-start(bf16[2,1,1,2,96,768]{5,4,3,2,1,0:T(8,128)(2,1)S(1)} %pad_maximum_fusion.5), channel_id=1, source_target_pairs={{0,8},{1,9},{2,10},{3,11},{4,12},{5,13},{6,14},{7,15},{8,0},{9,1},... | collective-permute-start | bytes 1769480 | tf_op jit(solution)/shard_map/ppermute | solution.py:537
  42.1 12.2 %collective-permute-start.8 = (bf16[2,2,1,1,96,768]{5,4,3,2,1,0:T(8,128)(2,1)S(1)}, bf16[2,2,1,1,96,768]{5,4,3,2,1,0:T(8,128)(2,1)S(1)}, u32[]{:S(2)}, u32[]{:S(2)}) collective-permute-start(bf16[2,2,1,1,96,768]{5,4,3,2,1,0:T(8,128)(2,1)S(1)} %pad_maximum_fusion.4), channel_id=1, source_target_pairs={{0,4},{1,5},{2,6},{3,7},{4,0},{5,1},{6,2},{7,3},{8,12},{9,13},{10,... | collective-permute-start | bytes 1769480 | tf_op jit(solution)/shard_map/ppermute | solution.py:537
  52.8 26.3 %collective-permute-start.14 = (bf16[2,2,1,2,96,768]{5,4,3,2,1,0:T(8,128)(2,1)S(1)}, bf16[2,2,1,2,96,768]{5,4,3,2,1,0:T(8,128)(2,1)S(1)}, u32[]{:S(2)}, u32[]{:S(2)}) collective-permute-start(bf16[2,2,1,2,96,768]{5,4,3,2,1,0:T(8,128)(2,1)S(1)} %pad_maximum_fusion.3), channel_id=1, source_target_pairs={{0,4},{1,5},{2,6},{3,7},{4,0},{5,1},{6,2},{7,3},{8,12},{9,13},{10,... | collective-permute-start | bytes 3538952 | tf_op jit(solution)/shard_map/ppermute | solution.py:537
  54.4 26.1 %collective-permute-start.9 = (bf16[2,2,2,1,96,768]{5,4,3,2,1,0:T(8,128)(2,1)S(1)}, bf16[2,2,2,1,96,768]{5,4,3,2,1,0:T(8,128)(2,1)S(1)}, u32[]{:S(2)}, u32[]{:S(2)}) collective-permute-start(bf16[2,2,2,1,96,768]{5,4,3,2,1,0:T(8,128)(2,1)S(1)} %pad_maximum_fusion.2), channel_id=1, source_target_pairs={{0,2},{1,3},{2,0},{3,1},{4,6},{5,7},{6,4},{7,5},{8,10},{9,11},{10,... | collective-permute-start | bytes 3538952 | tf_op jit(solution)/shard_map/ppermute | solution.py:537
  79.4 53.0 %collective-permute-start.15 = (bf16[1536,768]{1,0:T(8,128)(2,1)S(1)}, bf16[1536,768]{1,0:T(8,128)(2,1)}, u32[]{:S(2)}, u32[]{:S(2)}) collective-permute-start(bf16[1536,768]{1,0:T(8,128)(2,1)S(1)} %bitcast.56), channel_id=1, source_target_pairs={{0,1},{1,0},{2,3},{3,2},{4,5},{5,4},{6,7},{7,6},{8,9},{9,8},{10,11... | collective-permute-start | bytes 7077896 | tf_op jit(solution)/shard_map/ppermute | solution.py:537
  82.0 50.4 %collective-permute-start.10 = (bf16[1536,768]{1,0:T(8,128)(2,1)}, bf16[1536,768]{1,0:T(8,128)(2,1)}, u32[]{:S(2)}, u32[]{:S(2)}) collective-permute-start(bf16[1536,768]{1,0:T(8,128)(2,1)} %bitcast.3.refs_11_), channel_id=1, source_target_pairs={{0,1},{1,0},{2,3},{3,2},{4,5},{5,4},{6,7},{7,6},{8,9},{9,8},{10,11... | collective-permute-start | bytes 7077896 | tf_op jit(solution)/shard_map/ppermute | solution.py:537
  110.8 9.8 %collective-permute-start.2 = (bf16[192,512]{1,0:T(8,128)(2,1)}, bf16[192,512]{1,0:T(8,128)(2,1)S(1)}, u32[]{:S(2)}, u32[]{:S(2)}) collective-permute-start(bf16[192,512]{1,0:T(8,128)(2,1)} %get-tuple-element.38.rest_3_), channel_id=1, source_target_pairs={{0,3},{1,2},{2,1},{3,0},{4,7},{5,6},{6,5},{7,4},{8,11},{9,10},{10,... | collective-permute-start | bytes 589832 | tf_op jit(solution)/shard_map/ppermute | solution.py:537
  111.0 14.8 %collective-permute-start.3 = (bf16[192,768]{1,0:T(8,128)(2,1)S(1)}, bf16[192,768]{1,0:T(8,128)(2,1)S(1)}, u32[]{:S(2)}, u32[]{:S(2)}) collective-permute-start(bf16[192,768]{1,0:T(8,128)(2,1)S(1)} %fusion.8.refs_4_), channel_id=1, source_target_pairs={{0,1},{1,0},{2,3},{3,2},{4,5},{5,4},{6,7},{7,6},{8,9},{9,8},{10,11... | collective-permute-start | bytes 884744 | tf_op jit(solution)/shard_map/ppermute | solution.py:537
  117.3 10.6 %collective-permute-start.4 = (bf16[192,768]{1,0:T(8,128)(2,1)S(1)}, bf16[192,768]{1,0:T(8,128)(2,1)}, u32[]{:S(2)}, u32[]{:S(2)}) collective-permute-start(bf16[192,768]{1,0:T(8,128)(2,1)S(1)} %fusion.8.refs_4_), channel_id=1, source_target_pairs={{0,2},{1,3},{2,0},{3,1},{4,6},{5,7},{6,4},{7,5},{8,10},{9,11},{10,... | collective-permute-start | bytes 884744 | tf_op jit(solution)/shard_map/ppermute | solution.py:537
  121.3 11.1 %collective-permute-start.5 = (bf16[192,768]{1,0:T(8,128)(2,1)S(1)}, bf16[192,768]{1,0:T(8,128)(2,1)}, u32[]{:S(2)}, u32[]{:S(2)}) collective-permute-start(bf16[192,768]{1,0:T(8,128)(2,1)S(1)} %fusion.8.refs_4_), channel_id=1, source_target_pairs={{0,3},{1,2},{2,1},{3,0},{4,7},{5,6},{6,5},{7,4},{8,11},{9,10},{10,... | collective-permute-start | bytes 884744 | tf_op jit(solution)/shard_map/ppermute | solution.py:537
  193.7 9.5 %collective-permute-start.18 = (bf16[192,512]{1,0:T(8,128)(2,1)S(1)}, bf16[192,512]{1,0:T(8,128)(2,1)}, u32[]{:S(2)}, u32[]{:S(2)}) collective-permute-start(bf16[192,512]{1,0:T(8,128)(2,1)S(1)} %copy-done.23), channel_id=1, source_target_pairs={{0,3},{1,2},{2,1},{3,0},{4,7},{5,6},{6,5},{7,4},{8,11},{9,10},{10,... | collective-permute-start | bytes 589832 | tf_op jit(solution)/shard_map/ppermute | solution.py:537
  193.8 31.7 %collective-permute-start.21 = (bf16[192,768]{1,0:T(8,128)(2,1)S(1)}, bf16[192,768]{1,0:T(8,128)(2,1)}, u32[]{:S(2)}, u32[]{:S(2)}) collective-permute-start(bf16[192,768]{1,0:T(8,128)(2,1)S(1)} %convolution_convert_fusion.6), channel_id=1, source_target_pairs={{0,1},{1,0},{2,3},{3,2},{4,5},{5,4},{6,7},{7,6},{8,9},{9,8},{10,11... | collective-permute-start | bytes 884744 | tf_op jit(solution)/shard_map/ppermute | solution.py:537
  194.5 31.0 %collective-permute-start.22 = (bf16[192,768]{1,0:T(8,128)(2,1)S(1)}, bf16[192,768]{1,0:T(8,128)(2,1)}, u32[]{:S(2)}, u32[]{:S(2)}) collective-permute-start(bf16[192,768]{1,0:T(8,128)(2,1)S(1)} %convolution_convert_fusion.5), channel_id=1, source_target_pairs={{0,2},{1,3},{2,0},{3,1},{4,6},{5,7},{6,4},{7,5},{8,10},{9,11},{10,... | collective-permute-start | bytes 884744 | tf_op jit(solution)/shard_map/ppermute | solution.py:537
  196.3 29.2 %collective-permute-start.23 = (bf16[192,768]{1,0:T(8,128)(2,1)S(1)}, bf16[192,768]{1,0:T(8,128)(2,1)}, u32[]{:S(2)}, u32[]{:S(2)}) collective-permute-start(bf16[192,768]{1,0:T(8,128)(2,1)S(1)} %convolution_convert_fusion.4), channel_id=1, source_target_pairs={{0,3},{1,2},{2,1},{3,0},{4,7},{5,6},{6,5},{7,4},{8,11},{9,10},{10,... | collective-permute-start | bytes 884744 | tf_op jit(solution)/shard_map/ppermute | solution.py:537
  227.3 15.3 %collective-permute-start.24 = (bf16[1,2,2,96,768]{4,3,2,1,0:T(8,128)(2,1)S(1)}, bf16[1,2,2,96,768]{4,3,2,1,0:T(8,128)(2,1)S(1)}, u32[]{:S(2)}, u32[]{:S(2)}) collective-permute-start(bf16[1,2,2,96,768]{4,3,2,1,0:T(8,128)(2,1)S(1)} %bitcast.59), channel_id=1, source_target_pairs={{0,4},{1,5},{2,6},{3,7},{4,0},{5,1},{6,2},{7,3},{8,12},{9,13},{10,... | collective-permute-start | bytes 1769480 | tf_op jit(solution)/shard_map/ppermute | solution.py:537
  230.6 74.7 %collective-permute-start.40 = (bf16[1536,768]{1,0:T(8,128)(2,1)S(1)}, bf16[1536,768]{1,0:T(8,128)(2,1)S(1)}, u32[]{:S(2)}, u32[]{:S(2)}) collective-permute-start(bf16[1536,768]{1,0:T(8,128)(2,1)S(1)} %convolution_convert_fusion), channel_id=1, source_target_pairs={{0,1},{1,0},{2,3},{3,2},{4,5},{5,4},{6,7},{7,6},{8,9},{9,8},{10,11... | collective-permute-start | bytes 7077896 | tf_op jit(solution)/shard_map/ppermute | solution.py:537
  230.7 42.7 %collective-permute-start.31 = (f32[2,768]{1,0:T(2,128)S(1)}, f32[2,768]{1,0:T(2,128)S(1)}, u32[]{:S(2)}, u32[]{:S(2)}) collective-permute-start(f32[2,768]{1,0:T(2,128)S(1)} %fusion.21), channel_id=1, source_target_pairs={{0,2},{1,3},{2,0},{3,1},{4,6},{5,7},{6,4},{7,5},{8,10},{9,11},{10,... | collective-permute-start | bytes 18440 | tf_op jit(solution)/shard_map/ppermute | solution.py:537
  242.8 35.7 %collective-permute-start.25 = (bf16[1,1,2,96,768]{4,3,2,1,0:T(8,128)(2,1)S(1)}, bf16[1,1,2,96,768]{4,3,2,1,0:T(8,128)(2,1)S(1)}, u32[]{:S(2)}, u32[]{:S(2)}) collective-permute-start(bf16[1,1,2,96,768]{4,3,2,1,0:T(8,128)(2,1)S(1)} %select_convert_fusion.1), channel_id=1, source_target_pairs={{0,8},{1,9},{2,10},{3,11},{4,12},{5,13},{6,14},{7,15},{8,0},{9,1},... | collective-permute-start | bytes 884744 | tf_op jit(solution)/shard_map/ppermute | solution.py:537
  273.3 34.7 %collective-permute-start.35 = (bf16[1536,768]{1,0:T(8,128)(2,1)S(1)}, bf16[1536,768]{1,0:T(8,128)(2,1)S(1)}, u32[]{:S(2)}, u32[]{:S(2)}) collective-permute-start(bf16[1536,768]{1,0:T(8,128)(2,1)S(1)} %convolution_convert_fusion.2), channel_id=1, source_target_pairs={{0,1},{1,0},{2,3},{3,2},{4,5},{5,4},{6,7},{7,6},{8,9},{9,8},{10,11... | collective-permute-start | bytes 7077896 | tf_op jit(solution)/shard_map/ppermute | solution.py:537
  289.1 21.8 %collective-permute-start.19 = (bf16[2,768,512]{2,1,0:T(8,128)(2,1)S(1)}, bf16[2,768,512]{2,1,0:T(8,128)(2,1)S(1)}, u32[]{:S(2)}, u32[]{:S(2)}) collective-permute-start(bf16[2,768,512]{2,1,0:T(8,128)(2,1)S(1)} %copy-done.18), channel_id=1, source_target_pairs={{0,1},{1,0},{2,3},{3,2},{4,5},{5,4},{6,7},{7,6},{8,9},{9,8},{10,11... | collective-permute-start | bytes 4718600 | tf_op jit(solution)/shard_map/ppermute | solution.py:537
  296.0 8.9 %collective-permute-start.28 = (bf16[1,1,2,96,768]{4,3,2,1,0:T(8,128)(2,1)S(1)}, bf16[1,1,2,96,768]{4,3,2,1,0:T(8,128)(2,1)S(1)}, u32[]{:S(2)}, u32[]{:S(2)}) collective-permute-start(bf16[1,1,2,96,768]{4,3,2,1,0:T(8,128)(2,1)S(1)} %maximum_select_fusion.3), channel_id=1, source_target_pairs={{0,8},{1,9},{2,10},{3,11},{4,12},{5,13},{6,14},{7,15},{8,0},{9,1},... | collective-permute-start | bytes 884744 | tf_op jit(solution)/shard_map/ppermute | solution.py:537
  305.3 16.3 %collective-permute-start.29 = (bf16[1,2,2,96,768]{4,3,2,1,0:T(8,128)(2,1)S(1)}, bf16[1,2,2,96,768]{4,3,2,1,0:T(8,128)(2,1)S(1)}, u32[]{:S(2)}, u32[]{:S(2)}) collective-permute-start(bf16[1,2,2,96,768]{4,3,2,1,0:T(8,128)(2,1)S(1)} %maximum_select_fusion.1), channel_id=1, source_target_pairs={{0,4},{1,5},{2,6},{3,7},{4,0},{5,1},{6,2},{7,3},{8,12},{9,13},{10,... | collective-permute-start | bytes 1769480 | tf_op jit(solution)/shard_map/ppermute | solution.py:537
  306.0 38.9 %collective-permute-start.41 = (bf16[2,2,1,2,96,768]{5,4,3,2,1,0:T(8,128)(2,1)S(1)}, bf16[2,2,1,2,96,768]{5,4,3,2,1,0:T(8,128)(2,1)S(1)}, u32[]{:S(2)}, u32[]{:S(2)}) collective-permute-start(bf16[2,2,1,2,96,768]{5,4,3,2,1,0:T(8,128)(2,1)S(1)} %slice.267), channel_id=1, source_target_pairs={{0,4},{1,5},{2,6},{3,7},{4,0},{5,1},{6,2},{7,3},{8,12},{9,13},{10,... | collective-permute-start | bytes 3538952 | tf_op jit(solution)/shard_map/ppermute | solution.py:537
  308.7 37.2 %collective-permute-start.36 = (bf16[2,2,2,1,96,768]{5,4,3,2,1,0:T(8,128)(2,1)S(1)}, bf16[2,2,2,1,96,768]{5,4,3,2,1,0:T(8,128)(2,1)S(1)}, u32[]{:S(2)}, u32[]{:S(2)}) collective-permute-start(bf16[2,2,2,1,96,768]{5,4,3,2,1,0:T(8,128)(2,1)S(1)} %slice.268), channel_id=1, source_target_pairs={{0,2},{1,3},{2,0},{3,1},{4,6},{5,7},{6,4},{7,5},{8,10},{9,11},{10,... | collective-permute-start | bytes 3538952 | tf_op jit(solution)/shard_map/ppermute | solution.py:537
  311.1 53.3 %collective-permute-start.20 = (bf16[768,512]{1,0:T(8,128)(2,1)S(1)}, bf16[768,512]{1,0:T(8,128)(2,1)S(1)}, u32[]{:S(2)}, u32[]{:S(2)}) collective-permute-start(bf16[768,512]{1,0:T(8,128)(2,1)S(1)} %fusion.7), channel_id=1, source_target_pairs={{0,2},{1,3},{2,0},{3,1},{4,6},{5,7},{6,4},{7,5},{8,10},{9,11},{10,... | collective-permute-start | bytes 2359304 | tf_op jit(solution)/shard_map/ppermute | solution.py:537
  345.3 13.5 %collective-permute-start.42 = (bf16[2,1,1,2,96,768]{5,4,3,2,1,0:T(8,128)(2,1)S(1)}, bf16[2,1,1,2,96,768]{5,4,3,2,1,0:T(8,128)(2,1)S(1)}, u32[]{:S(2)}, u32[]{:S(2)}) collective-permute-start(bf16[2,1,1,2,96,768]{5,4,3,2,1,0:T(8,128)(2,1)S(1)} %slice.269), channel_id=1, source_target_pairs={{0,8},{1,9},{2,10},{3,11},{4,12},{5,13},{6,14},{7,15},{8,0},{9,1},... | collective-permute-start | bytes 1769480 | tf_op jit(solution)/shard_map/ppermute | solution.py:537
  346.3 14.1 %collective-permute-start.37 = (bf16[2,2,1,1,96,768]{5,4,3,2,1,0:T(8,128)(2,1)S(1)}, bf16[2,2,1,1,96,768]{5,4,3,2,1,0:T(8,128)(2,1)S(1)}, u32[]{:S(2)}, u32[]{:S(2)}) collective-permute-start(bf16[2,2,1,1,96,768]{5,4,3,2,1,0:T(8,128)(2,1)S(1)} %slice.270), channel_id=1, source_target_pairs={{0,4},{1,5},{2,6},{3,7},{4,0},{5,1},{6,2},{7,3},{8,12},{9,13},{10,... | collective-permute-start | bytes 1769480 | tf_op jit(solution)/shard_map/ppermute | solution.py:537
  358.9 13.6 %collective-permute-start.43 = (bf16[1,1,1,2,96,768]{5,4,3,2,1,0:T(8,128)(2,1)S(1)}, bf16[1,1,1,2,96,768]{5,4,3,2,1,0:T(8,128)(2,1)}, u32[]{:S(2)}, u32[]{:S(2)}) collective-permute-start(bf16[1,1,1,2,96,768]{5,4,3,2,1,0:T(8,128)(2,1)S(1)} %slice.271), channel_id=1, source_target_pairs={{0,16},{1,17},{2,18},{3,19},{4,20},{5,21},{6,22},{7,23},{8,24},{9,... | collective-permute-start | bytes 884744 | tf_op jit(solution)/shard_map/ppermute | solution.py:537
  361.2 13.9 %collective-permute-start.38 = (bf16[2,1,1,1,96,768]{5,4,3,2,1,0:T(8,128)(2,1)}, bf16[2,1,1,1,96,768]{5,4,3,2,1,0:T(8,128)(2,1)}, u32[]{:S(2)}, u32[]{:S(2)}) collective-permute-start(bf16[2,1,1,1,96,768]{5,4,3,2,1,0:T(8,128)(2,1)} %slice.272), channel_id=1, source_target_pairs={{0,8},{1,9},{2,10},{3,11},{4,12},{5,13},{6,14},{7,15},{8,0},{9,1},... | collective-permute-start | bytes 884744 | tf_op jit(solution)/shard_map/ppermute | solution.py:537
  (43 other events, 417.8 us)
